TPU v7x, 512 devices: a whole 4x8x8 slice. The times are simulated.
512 devices in a mesh: prompt: 4 (over x), ctx: 128 (over z, y, core).
Axes of the slice: x: 4, y: 8, z: 8, core: 2. Of those that a mesh axis runs over, the one named last changes fastest.
Arguments:
- queries: bfloat16 [4, 512, 32, 128], P('prompt', 'ctx'), may hold values from -8 to 8
- prefix_keys: bfloat16 [4, 32768, 2, 128], P('prompt', 'ctx'), may hold values from -16 to 16
- prompt_value_rows: bfloat16 [4, 32768, 2, 128], P('prompt', 'ctx'), may hold values from -6 to 6
- generated_keys: bfloat16 [4, 512, 32, 2, 128], P('prompt', 'ctx'), may hold values from -16 to 16
- generated_values: bfloat16 [4, 512, 32, 2, 128], P('prompt', 'ctx'), may hold values from -6 to 6
- suffix_lengths: int32 [4, 512], P('prompt', 'ctx'), may hold values from 1 to 32, as said below
- hidden_rows: bfloat16 [4, 512, 2048], P('prompt', 'ctx'), may hold values from -6 to 6
- routed_experts: int32 [512, 4, 8], P('ctx'), may hold values from 0 to 127, all different within a row; in each aligned block of 16 rows (0 to 15, 16 to 31, ..., all dimensions but the last counted through in order) at most 2 rows name the same one
- routing_weights: float32 [512, 4, 8], P('ctx'), may hold values from 0.05 to 0.3
- gate_weight: bfloat16 [128, 768, 2048], P('ctx', 'prompt'), may hold values from -0.125 to 0.125
- up_weight: bfloat16 [128, 768, 2048], P('ctx', 'prompt'), may hold values from -0.125 to 0.125
- down_weight: bfloat16 [128, 768, 2048], P('ctx', 'prompt'), may hold values from -0.21875 to 0.21875
Outputs:
- attended: bfloat16 [4, 512, 32, 128], P('prompt', 'ctx')
- expert_mix: bfloat16 [4, 512, 2048], P('prompt', 'ctx')
Inputs may be any that keep to these rules, and one draw needn't show every extreme that they name: `suffix_lengths`: some sample's suffix has exactly 32 live positions. `routed_experts`: each row names 8 different experts. In the rows of one index of ctx (aligned blocks of 16 rows, samples major), no expert is named by more than 2 rows, a bound that some block reaches.
All inputs are finite; a program needn't handle non-finite values.
Results may differ from a plain program's by a relative error of at most 0.013.
Values may be sent and summed in bfloat16 or wider, within the bound.
No kernel may reach another device: no remote copies, remote signals or barrier semaphores. Data moves between devices by JAX's collectives and lax.ppermute only.
A program may use at most 128 MiB of HBM per device.

v0:
```python
import math

import jax
import jax.numpy as jnp
from jax import lax
from jax.sharding import PartitionSpec as P


def block_view(gathered, key_cache):
    sample_count = gathered.shape[1]
    head_count = gathered.shape[2]
    head_size = gathered.shape[3]
    shared_heads = key_cache.shape[1]
    rows_per_block = math.gcd(sample_count, 16)
    return gathered.reshape(
        sample_count // rows_per_block,
        rows_per_block,
        shared_heads,
        head_count // shared_heads,
        head_size,
    )


def add_sources(terms):
    return (jnp.sum(terms[0], axis=1), jnp.sum(terms[1], axis=1))


def row_product(left, right):
    return lax.dot_general(
        left, right, (((1,), (1,)), ((), ())), preferred_element_type=jnp.float32
    )


def suffix_merge(queries, summed, totals, peaks, generated_keys, generated_values, suffix_lengths):
    own_count = queries.shape[1]
    head_count = queries.shape[2]
    head_size = queries.shape[3]
    trailing_keys = generated_keys[0]
    trailing_values = generated_values[0]
    shared_heads = trailing_keys.shape[2]
    longest = trailing_keys.shape[1]
    score_scale = head_size ** (-0.5)
    own_query = queries[0].reshape(own_count, shared_heads, head_count // shared_heads, head_size)
    scores = (
        jnp.einsum("bgqd,bjgd->bgqj", own_query, trailing_keys, preferred_element_type=jnp.float32)
        * score_scale
    )
    active = (jnp.arange(longest, dtype=jnp.int32)[None, :] < suffix_lengths[0][:, None])[
        :, None, None, :
    ]
    scores = jnp.where(active, scores, -1e30)
    highest = jnp.max(scores, axis=3)
    exp_terms = jnp.where(active, jnp.exp(scores - highest[..., None]), 0.0)
    suffix_total = jnp.sum(exp_terms, axis=3).reshape(own_count, head_count)
    suffix_sum = jnp.einsum(
        "bgqj,bjgd->bgqd",
        exp_terms.astype(jnp.bfloat16),
        trailing_values,
        preferred_element_type=jnp.float32,
    )
    suffix_sum = suffix_sum.reshape(own_count, head_count, head_size)
    highest = highest.reshape(own_count, head_count)
    highest_all = jnp.maximum(peaks, highest)
    prompt_factor = jnp.exp(peaks - highest_all)
    suffix_factor = jnp.exp(highest - highest_all)
    numerator = summed * prompt_factor[..., None] + suffix_sum * suffix_factor[..., None]
    denominator = totals * prompt_factor + suffix_total * suffix_factor
    return (
        (numerator / denominator[..., None])
        .reshape(1, own_count, head_count, head_size)
        .astype(jnp.bfloat16)
    )


def dispatch_plan(chosen, experts, capacity):
    matches = (chosen[:, :, None] == jnp.arange(experts, dtype=jnp.int32)[None, None, :]).astype(
        jnp.int32
    )
    per_row = jnp.sum(matches, axis=1)
    earlier = jnp.cumsum(per_row, axis=0) - per_row
    slot_index = jnp.sum(matches * earlier[:, None, :], axis=2)
    return chosen * capacity + slot_index


def body(
    queries,
    prefix_keys,
    prompt_value_rows,
    generated_keys,
    generated_values,
    suffix_lengths,
    hidden_rows,
    routed_experts,
    routing_weights,
    gate_weight,
    up_weight,
    down_weight,
):
    prompt_parts = lax.axis_size("prompt")
    own_samples = hidden_rows.shape[1]
    model_width = hidden_rows.shape[2]
    column = lax.all_gather(
        hidden_rows.reshape(own_samples, 1, model_width), "prompt", axis=1, tiled=True
    )
    row_matrix = column.reshape(own_samples * prompt_parts, model_width)
    chosen_count = routed_experts.shape[2]
    chosen = routed_experts.reshape(-1, chosen_count)
    gate_share = routing_weights.reshape(-1, chosen_count)
    row_total = row_matrix.shape[0]
    experts = gate_weight.shape[0] * lax.axis_size("ctx")
    capacity = min(row_total, -(-(row_total * chosen_count) // experts) + 1)
    target = dispatch_plan(chosen, experts, capacity)
    lane_index = jnp.arange(experts * capacity, dtype=jnp.int32)
    lane_hits = jnp.any(target[None, :, :] == lane_index[:, None, None], axis=2)
    row_numbers = jnp.arange(row_total, dtype=jnp.int32)
    lane_row = jnp.min(jnp.where(lane_hits, row_numbers[None, :], row_total), axis=1)
    padded = jnp.concatenate([row_matrix, jnp.zeros((1, model_width), jnp.bfloat16)], axis=0)
    outgoing = jnp.take(padded, lane_row, axis=0).reshape(experts, capacity, model_width)
    arrived = lax.all_to_all(outgoing, "ctx", split_axis=0, concat_axis=0, tiled=True)
    sources = arrived.shape[0]
    slot_count = arrived.shape[1]
    tokens_in = arrived.reshape(sources * slot_count, model_width)
    gate_act = row_product(tokens_in, gate_weight[0])
    up_act = row_product(tokens_in, up_weight[0])
    activation = (jax.nn.silu(gate_act) * up_act).astype(jnp.bfloat16)
    part_out = jnp.dot(activation, down_weight[0], preferred_element_type=jnp.float32).astype(
        jnp.bfloat16
    )
    returned = lax.all_to_all(
        part_out.reshape(sources, slot_count, model_width),
        "ctx",
        split_axis=0,
        concat_axis=0,
        tiled=True,
    )
    flat_back = returned.reshape(experts * capacity, returned.shape[2])
    picked = jnp.take(flat_back, target.reshape(-1), axis=0).reshape(
        row_total, chosen_count, returned.shape[2]
    )
    weighted = jnp.sum(picked.astype(jnp.float32) * gate_share[:, :, None], axis=1)
    spread = weighted.reshape(own_samples, prompt_parts, 1, model_width)
    joined = lax.all_to_all(
        spread.astype(jnp.bfloat16), "prompt", split_axis=1, concat_axis=2, tiled=True
    ).astype(spread.dtype)
    expert_mix = jnp.sum(joined, axis=2).reshape(1, own_samples, model_width).astype(jnp.bfloat16)
    gathered = lax.all_gather(queries, "ctx", axis=1, tiled=True)
    key_cache = prefix_keys[0]
    value_cache = prompt_value_rows[0]
    blocks = block_view(gathered, key_cache)
    sample_count = gathered.shape[1]
    head_count = gathered.shape[2]
    head_size = gathered.shape[3]
    score_scale = head_size ** (-0.5)
    scores = lax.map(
        lambda block_of_queries: jnp.einsum(
            "bgqd,tgd->bgqt", block_of_queries, key_cache, preferred_element_type=jnp.float32
        )
        * score_scale,
        blocks,
    )
    local_peak = jnp.max(scores, axis=4)
    common_peak = lax.pmax(local_peak.astype(jnp.bfloat16), "ctx").astype(local_peak.dtype)

    def shifted(block_inputs):
        block_scores, block_peak = block_inputs
        exp_terms = jnp.exp(block_scores - block_peak[..., None])
        block_sum = jnp.einsum(
            "bgqt,tgd->bgqd",
            exp_terms.astype(jnp.bfloat16),
            value_cache,
            preferred_element_type=jnp.float32,
        )
        return (block_sum, jnp.sum(exp_terms, axis=3))

    summed, totals = lax.map(shifted, (scores, common_peak))
    summed, totals = add_sources(
        (
            lax.all_to_all(
                summed.reshape(sample_count, 1, head_count, head_size).astype(jnp.bfloat16),
                "ctx",
                split_axis=0,
                concat_axis=1,
                tiled=True,
            ).astype(jnp.float32),
            lax.all_to_all(
                totals.reshape(sample_count, 1, head_count).astype(jnp.bfloat16),
                "ctx",
                split_axis=0,
                concat_axis=1,
                tiled=True,
            ).astype(jnp.float32),
        )
    )
    own_count = queries.shape[1]
    peaks = lax.dynamic_slice_in_dim(
        common_peak.reshape(sample_count, head_count),
        lax.axis_index("ctx") * own_count,
        own_count,
        0,
    )
    attended = suffix_merge(
        queries, summed, totals, peaks, generated_keys, generated_values, suffix_lengths
    )
    return (attended, expert_mix)


def solution(mesh):
    placed = (
        P("prompt", "ctx", None, None),
        P("prompt", "ctx", None, None),
        P("prompt", "ctx", None, None),
        P("prompt", "ctx", None, None, None),
        P("prompt", "ctx", None, None, None),
        P("prompt", "ctx"),
        P("prompt", "ctx", None),
        P("ctx", None, None),
        P("ctx", None, None),
        P("ctx", "prompt", None),
        P("ctx", "prompt", None),
        P("ctx", "prompt", None),
    )
    return jax.shard_map(
        body,
        mesh=mesh,
        in_specs=placed,
        out_specs=(P("prompt", "ctx", None, None), P("prompt", "ctx", None)),
        check_vma=False,
    )
```

profile of v0, /device:TPU:1, one launch (start us, length us, event | category | flops | bytes accessed | tf_op | source)
XLA Modules:
  0.0 942.1 jit_solution(1921240314477519178)
XLA Ops:
  8.8 10.4 %all-gather = bf16[1,4,8192]{2,1,0:T(4,128)(2,1)S(1)} all-gather(bf16[1,4,2048]{2,1,0:T(4,128)(2,1)} %param.22), channel_id=2, replica_groups=mesh['prompt'=4,'ctx'=128] {'prompt'}, dimensions={2}, use_global_device_ids=true | all-gather | bytes 81920 | tf_op jit(solution)/shard_map/all_gather | solution.py:102
  24.5 51.4 %all_to_all.37 = bf16[128,2,2048]{2,1,0:T(2,128)(2,1)S(1)} all-to-all(bf16[128,2,2048]{2,1,0:T(2,128)(2,1)S(1)} %broadcast_select_fusion), channel_id=1, replica_groups=mesh['prompt'=4,'ctx'=128] {'ctx'}, dimensions={0} | all-to-all | bytes 2097152 | tf_op jit(solution)/shard_map/all_to_all | solution.py:119
  78.0 2.6 convolution_convert_fusion
  82.2 6.7 all-to-all-start.3
  89.2 33.2 %all-to-all-done.3 = bf16[128,2,2048]{2,1,0:T(2,128)(2,1)S(1)} async-done(((bf16[128,2,2048]{2,1,0:T(2,128)(2,1)}), bf16[128,2,2048]{2,1,0:T(2,128)(2,1)S(1)}, u32[]{:S(2)}, u32[]{:S(2)}) %all-to-all-start.3) | async-done | bytes 1048608 | tf_op jit(solution)/shard_map/all_to_all | solution.py:129
  125.5 3.8 all-to-all-start.4
  129.3 3.6 all-gather.3.cloned.1.call-done
  132.9 62.2 %while.22 = (s32[]{:T(128)}, f32[32,16,2,16,256]{4,3,1,2,0:T(8,128)}, bf16[32,16,2,16,128]{4,3,2,1,0:T(8,128)(2,1)}, bf16[256,2,128]{2,0,1:T(8,128)(2,1)S(1)}, s32[]{:T(128)}) while((s32[]{:T(128)}, f32[32,16,2,16,256]{4,3,1,2,0:T(8,128)}, bf16[32,16,2,16,128]{4,3,2,1,0:T(8,128)(2,1)}, bf16[256,2,128]{2,0,1:T(8,128)(2,1)S(1)}, s32[]{:T(128)}) %tuple.54), condition=%wide.region_1.0_spmd, body=%wide.region_0.0_spmd.sunk | while | flops 33685504 | bytes 787517 | solution.py:154
  134.8 1.9 fusion.53
  136.8 2.0 fusion.53
  138.7 1.9 fusion.53
  146.5 1.9 fusion.53
  150.3 2.0 fusion.53
  152.3 1.9 fusion.53
  156.2 1.9 fusion.53
  158.1 2.0 fusion.53
  162.0 1.9 fusion.53
  163.9 2.0 fusion.53
  165.9 2.0 fusion.53
  171.8 2.0 fusion.53
  173.7 1.9 fusion.53
  177.6 1.9 fusion.53
  179.5 2.0 fusion.53
  181.5 2.0 fusion.53
  187.3 1.9 fusion.53
  195.1 8.1 reduce_max.18
  203.1 488.6 %pmax.7 = bf16[32,16,2,16]{3,1,2,0:T(8,128)(2,1)S(1)} all-reduce(bf16[32,16,2,16]{3,1,2,0:T(8,128)(2,1)S(1)} %reduce_max.18), channel_id=1, replica_groups=mesh['prompt'=4,'ctx'=128] {'ctx'}, use_global_device_ids=true, to_apply=%region_3.4 | all-reduce | flops 16384 | bytes 65536 | tf_op jit(solution)/shard_map/pmax | solution.py:162
  691.8 107.3 %while.23 = (s32[]{:T(128)}, bf16[32,16,2,16,128]{4,3,2,1,0:T(8,128)(2,1)}, bf16[32,16,2,16]{3,1,2,0:T(8,128)(2,1)S(1)}, f32[32,16,2,16,256]{4,3,1,2,0:T(8,128)}...) while((s32[]{:T(128)}, bf16[32,16,2,16,128]{4,3,2,1,0:T(8,128)(2,1)}, ...), condition=%wide.region_6.7_spmd, body=%wide.region_4.6_spmd.sunk | while | flops 34078208 | bytes 1599577 | solution.py:175
  799.4 28.3 %all_to_all.38 = bf16[512,1,32]{2,1,0:T(2,128)(2,1)S(1)} all-to-all(bf16[512,1,32]{2,1,0:T(2,128)(2,1)S(1)} %reshape.297), channel_id=1, replica_groups=mesh['prompt'=4,'ctx'=128] {'ctx'}, dimensions={0} | all-to-all | bytes 65536 | tf_op jit(solution)/shard_map/all_to_all | solution.py:185
  827.7 6.8 all-to-all-start
  837.1 94.5 %all-to-all-done = bf16[512,1,32,128]{3,2,1,0:T(8,128)(2,1)} async-done(((bf16[512,1,32,128]{3,2,1,0:T(8,128)(2,1)}), bf16[512,1,32,128]{3,2,1,0:T(8,128)(2,1)}, u32[]{:S(2)}, u32[]{:S(2)}) %all-to-all-start) | async-done | bytes 4194336 | tf_op jit(solution)/shard_map/all_to_all | solution.py:178
  931.6 2.9 convert_reduce_fusion
  (246 shorter events, 152.3 us)
Async XLA Ops:
  7.2 70.8 %copy-start = (bf16[1,192,2048]{2,1,0:T(8,128)(2,1)S(1)}, bf16[1,192,2048]{2,1,0:T(8,128)(2,1)}, u32[]{:S(2)}) copy-start(bf16[1,192,2048]{2,1,0:T(8,128)(2,1)} %param.27) | copy-start | bytes 2359300
  7.2 125.7 %all-gather.3.cloned.1.call-start = ((), (), s32[]{:S(2)}) async-start(), calls=%async_computation.5 | async-start | bytes 4227072 | tf_op jit(solution)/shard_map/all_gather | solution.py:146
  78.0 11.0 %copy-start.2 = (bf16[1,256,2,128]{3,2,1,0:T(2,128)(2,1)S(1)}, bf16[1,256,2,128]{3,2,1,0:T(2,128)(2,1)}, u32[]{:S(2)}) copy-start(bf16[1,256,2,128]{3,2,1,0:T(2,128)(2,1)} %param.17) | copy-start | bytes 393220
  78.0 11.1 %copy-start.1 = (s32[4,4,8]{2,1,0:T(4,128)S(1)}, s32[4,4,8]{2,1,0:T(4,128)}, u32[]{:S(2)}) copy-start(s32[4,4,8]{2,1,0:T(4,128)} %param.23) | copy-start | bytes 1540
  80.6 8.4 copy-start.3
  82.2 40.3 %all-to-all-start.3 = ((bf16[128,2,2048]{2,1,0:T(2,128)(2,1)}), bf16[128,2,2048]{2,1,0:T(2,128)(2,1)S(1)}, u32[]{:S(2)}, u32[]{:S(2)}) async-start(bf16[128,2,2048]{2,1,0:T(2,128)(2,1)} %reshape.272), calls=%async_computation.3 | async-start | bytes 2097152 | tf_op jit(solution)/shard_map/all_to_all | solution.py:129
  88.9 35.0 %copy-start.6 = (f32[4,4,8]{2,1,0:T(4,128)S(1)}, f32[4,4,8]{2,1,0:T(4,128)}, u32[]{:S(2)}) copy-start(f32[4,4,8]{2,1,0:T(4,128)} %param.24) | copy-start | bytes 1540
  125.5 673.9 %all-to-all-start.4 = ((bf16[4,4,1,2048]{3,0,2,1:T(4,128)(2,1)}), bf16[4,4,1,2048]{3,0,2,1:T(4,128)(2,1)S(1)}, u32[]{:S(2)}, u32[]{:S(2)}) async-start(bf16[4,4,1,2048]{3,0,2,1:T(4,128)(2,1)} %copy.85), calls=%async_computation.4 | async-start | bytes 131072 | tf_op jit(solution)/shard_map/all_to_all | solution.py:142
  827.7 6.8 copy-start.8
  827.7 6.9 copy-start.4
  827.7 6.9 copy-start.5
  827.7 7.5 copy-start.7
  827.7 103.9 %all-to-all-start = ((bf16[512,1,32,128]{3,2,1,0:T(8,128)(2,1)}), bf16[512,1,32,128]{3,2,1,0:T(8,128)(2,1)}, u32[]{:S(2)}, u32[]{:S(2)}) async-start(bf16[512,1,32,128]{3,2,1,0:T(8,128)(2,1)} %bitcast.109), calls=%async_computation | async-start | bytes 8388608 | tf_op jit(solution)/shard_map/all_to_all | solution.py:178
Sparse Core Ops, SparseCore 0:
  11.1 121.7 all-gather.2
where the time goes:
time: 953 us; the launch traced here: 942 us
  blocking collectives  579 us (61%)
  waiting for transfers between devices  132 us (14%)
  matrix products  109 us (11%)
  other arithmetic  59.4 us (6%)
  local copies, waits for them, and re-layouts  29.5 us (3%)
  starting transfers between devices  17.3 us (2%)
  between operations  14.4 us (2%)
    pmax x1, blocking collectives, body(): lax.pmax(local_peak.astype(jnp.bfloat16), 'ctx').astype(local_peak.dtype)  489 us
    all_to_all x1, waiting for transfers between devices, body(): lax.all_to_all(summed.reshape(sample_count, 1, head_count, head_size).ast...  94.5 us
    dot_general x32, matrix products, body(): jnp.einsum('bgqd,tgd->bgqt', block_of_queries, key_cache, preferred_eleme...  62.1 us
    all_to_all x1, blocking collectives, body(): lax.all_to_all(outgoing, 'ctx', split_axis=0, concat_axis=0, tiled=True)  51.4 us
    dot_general x32, matrix products, shifted(): jnp.einsum('bgqt,tgd->bgqd', exp_terms.astype(jnp.bfloat16), value_cache,...  42.6 us
    reduce_sum x32, other arithmetic, shifted(): return (block_sum, jnp.sum(exp_terms, axis=3))  41.5 us
    all_to_all x1, waiting for transfers between devices, body(): lax.all_to_all(part_out.reshape(sources, slot_count, model_width), 'ctx',...  33.2 us
    all_to_all x1, blocking collectives, body(): lax.all_to_all(totals.reshape(sample_count, 1, head_count).astype(jnp.bfl...  28.3 us
  transfers between devices with their start and end apart: 4, of which 3 were waited for; matrix products, arithmetic and copies ran while one was open for 21% of the time, Pallas kernels for 0%

commit v1 on v0

v1 whole, which is shorter than its diff:
```python
import math

import jax
import jax.numpy as jnp
from jax import lax
from jax.experimental import pallas as pl
from jax.experimental.pallas import tpu as pltpu
from jax.sharding import Mesh
from jax.sharding import PartitionSpec as P

BF16 = jnp.bfloat16
F32 = jnp.float32
LOG2E = 1.4426950408889634
EXTRA = 16


def three_parts(value):
    high = value.astype(BF16)
    rest = value - high.astype(F32)
    middle = rest.astype(BF16)
    low = (rest - middle.astype(F32)).astype(BF16)
    return high, middle, low


def attention_kernel(scale, q_ref, kv_ref, out_ref, vaug_ref):
    samples, groups, per_group, width = q_ref.shape
    dests = out_ref.shape[0]
    positions = kv_ref.shape[0] * kv_ref.shape[3]

    @pl.when(pl.program_id(0) == 0)
    def _():
        for g in range(groups):
            vaug_ref[g, :, :width] = kv_ref[:, 1, g].reshape(positions, width)
            vaug_ref[g, :, width:] = jnp.ones((positions, width), BF16)

    outs, logs = [], []
    for g in range(groups):
        rows = q_ref[:, g].reshape(samples * per_group, width)
        keys = kv_ref[:, 0, g].reshape(positions, width)
        scores = lax.dot_general(rows, keys, (((1,), (1,)), ((), ())), preferred_element_type=F32)
        peak = jnp.max(scores, axis=1, keepdims=True)
        probs = jnp.exp2((scores - peak) * (scale * LOG2E)).astype(BF16)
        summed = jnp.dot(probs, vaug_ref[g], preferred_element_type=F32)
        total = summed[:, width:]
        outs.append((summed[:, :width] / total).astype(BF16).reshape(samples, 1, per_group, width))
        logs.append((peak * scale + jnp.log(total)).reshape(samples, 1, per_group, width))
    out_ref[:, : groups * per_group * (samples // dests), :] = jnp.concatenate(outs, axis=1).reshape(
        dests, samples // dests * groups * per_group, width
    )
    joined = jnp.concatenate(logs, axis=1).reshape(dests, samples // dests * groups * per_group, width)
    for d in range(dests):
        line = jnp.transpose(joined[d])[0:1, :]
        parts = jnp.concatenate(
            [part.astype(F32) for part in three_parts(line)] + [jnp.zeros((EXTRA - 3, width), F32)], axis=0
        )
        out_ref[d, width:, :] = parts.astype(BF16)


def attention(q_all, kv_all, scale):
    sources, own, heads, width = q_all.shape
    groups = kv_all.shape[2]
    samples = sources * own
    dests_per_step = 4
    steps = sources // dests_per_step
    positions = kv_all.shape[0] * kv_all.shape[3]
    pairs = samples * heads * positions
    q_view = q_all.reshape(samples, groups, heads // groups, width)
    return pl.pallas_call(
        lambda *refs: attention_kernel(scale, *refs),
        grid=(steps,),
        in_specs=[
            pl.BlockSpec((samples // steps, groups, heads // groups, width), lambda i: (i, 0, 0, 0)),
            pl.BlockSpec(kv_all.shape, lambda i: (0, 0, 0, 0, 0)),
        ],
        out_specs=pl.BlockSpec((dests_per_step, own * heads + EXTRA, width), lambda i: (i, 0, 0)),
        out_shape=jax.ShapeDtypeStruct((sources, own * heads + EXTRA, width), BF16),
        scratch_shapes=[pltpu.VMEM((groups, positions, 2 * width), BF16)],
        compiler_params=pltpu.CompilerParams(vmem_limit_bytes=40 * 1024 * 1024),
        cost_estimate=pl.CostEstimate(
            flops=6 * pairs * width, bytes_accessed=2 * (kv_all.size + 2 * q_all.size), transcendentals=pairs
        ),
        name="prompt_attention",
    )(q_view, kv_all)


def expert_kernel(place_ref, piece0, piece1, piece2, piece3, gate_ref, up_ref, down_ref, *out_refs):
    parts = len(out_refs)
    width = piece0.shape[1]
    place = place_ref[0]
    gate = up = None
    for shift, piece in enumerate((piece0, piece1, piece2, piece3)):
        block = lax.rem(place - shift + parts, parts)
        columns = pl.ds(pl.multiple_of(block * width, width), width)
        dims = (((1,), (1,)), ((), ()))
        more_gate = lax.dot_general(piece[...], gate_ref[:, columns], dims, preferred_element_type=F32)
        more_up = lax.dot_general(piece[...], up_ref[:, columns], dims, preferred_element_type=F32)
        gate = more_gate if gate is None else gate + more_gate
        up = more_up if up is None else up + more_up
    act = (gate / (1.0 + jnp.exp(-gate)) * up).astype(BF16)
    for shift, out_ref in enumerate(out_refs):
        block = lax.rem(place + shift, parts)
        columns = pl.ds(pl.multiple_of(block * width, width), width)
        out_ref[...] = jnp.dot(act, down_ref[:, columns], preferred_element_type=F32).astype(BF16)


def expert_parts(place, pieces, gate_weight, up_weight, down_weight):
    rows, width = pieces[0].shape
    parts = len(pieces)
    vmem = pl.BlockSpec(memory_space=pltpu.VMEM)
    return pl.pallas_call(
        expert_kernel,
        in_specs=[pl.BlockSpec(memory_space=pltpu.SMEM)] + [vmem] * (parts + 3),
        out_specs=[vmem] * parts,
        out_shape=[jax.ShapeDtypeStruct((rows, width), BF16)] * parts,
        compiler_params=pltpu.CompilerParams(vmem_limit_bytes=24 * 1024 * 1024),
        cost_estimate=pl.CostEstimate(
            flops=6 * rows * width * parts * gate_weight.shape[0],
            bytes_accessed=6 * gate_weight.size + 16 * rows * width,
            transcendentals=rows * gate_weight.shape[0],
        ),
        name="expert_parts",
    )(place, *pieces, gate_weight, up_weight, down_weight)


def suffix_part(own_query, keys, values, lengths, scale):
    scores = jnp.einsum("bgqd,bjgd->bgqj", own_query, keys, preferred_element_type=F32) * scale
    live = (jnp.arange(keys.shape[1], dtype=jnp.int32)[None, :] < lengths[:, None])[:, None, None, :]
    scores = jnp.where(live, scores, -1e30)
    peak = jnp.max(scores, axis=3)
    terms = jnp.where(live, jnp.exp(scores - peak[..., None]), 0.0)
    total = jnp.sum(terms, axis=3)
    summed = jnp.einsum("bgqj,bjgd->bgqd", terms.astype(BF16), values, preferred_element_type=F32)
    return summed / total[..., None], peak + jnp.log(total)


def body(
    queries,
    prefix_keys,
    prompt_value_rows,
    generated_keys,
    generated_values,
    suffix_lengths,
    hidden_rows,
    routed_experts,
    routing_weights,
    gate_weight,
    up_weight,
    down_weight,
):
    prompts = lax.axis_size("x")
    place = lax.axis_index("x")
    own, heads, width = queries.shape[1:]
    groups = prefix_keys.shape[2]
    scale = width ** (-0.5)

    kv = jnp.stack([prefix_keys[0].transpose(1, 0, 2), prompt_value_rows[0].transpose(1, 0, 2)])
    kv_all = lax.all_gather(kv, "z", axis=0, tiled=False)
    q_all = lax.all_gather(queries[0], ("y", "c"), axis=0, tiled=False)

    features = hidden_rows.shape[2]
    quarter = features // prompts
    row_quarter = lax.all_to_all(
        hidden_rows.reshape(own, 1, features), "x", split_axis=2, concat_axis=1, tiled=True
    ).reshape(own * prompts, quarter)
    rows = own * prompts
    top = routed_experts.shape[2]
    experts = lax.axis_size(("z", "y", "c")) * gate_weight.shape[0]
    slots = min(2, rows)
    chosen = routed_experts.reshape(rows, top)
    shares = routing_weights.reshape(rows, top)
    matches = chosen[:, :, None] == jnp.arange(experts, dtype=jnp.int32)[None, None, :]
    named = jnp.any(matches, axis=1)
    share_of = jnp.sum(jnp.where(matches, shares[:, :, None], 0.0), axis=1)
    earlier = jnp.cumsum(named.astype(jnp.int32), axis=0) - named.astype(jnp.int32)
    slot_is = named[:, :, None] & (earlier[:, :, None] == jnp.arange(slots, dtype=jnp.int32)[None, None, :])
    sent = jnp.einsum("rej,rd->ejd", slot_is.astype(BF16), row_quarter, preferred_element_type=F32).astype(BF16)
    arrived = lax.all_to_all(sent, ("z", "y", "c"), split_axis=0, concat_axis=0, tiled=True)
    piece = arrived.reshape(experts * slots, quarter)
    pieces = [piece] + [
        lax.ppermute(piece, "x", [(i, (i + s) % prompts) for i in range(prompts)]) for s in range(1, prompts)
    ]
    parts = expert_parts(
        place.astype(jnp.int32).reshape(1), pieces, gate_weight[0], up_weight[0], down_weight[0]
    )
    received = [parts[0]] + [
        lax.ppermute(parts[s], "x", [(i, (i + s) % prompts) for i in range(prompts)]) for s in range(1, prompts)
    ]
    expert_sum = sum(r.astype(F32) for r in received).astype(BF16)
    returned = lax.all_to_all(
        expert_sum.reshape(experts, slots, quarter), ("z", "y", "c"), split_axis=0, concat_axis=0, tiled=True
    ).reshape(experts * slots, quarter)
    share_slots = jnp.where(slot_is, share_of[:, :, None], 0.0).reshape(rows, experts * slots)
    share_high = share_slots.astype(BF16)
    share_low = (share_slots - share_high.astype(F32)).astype(BF16)
    mixed = jnp.dot(jnp.concatenate([share_high, share_low]), returned, preferred_element_type=F32)
    mixed = (mixed[:rows] + mixed[rows:]).astype(BF16).reshape(own, prompts, quarter)
    expert_mix = lax.all_to_all(mixed, "x", split_axis=1, concat_axis=2, tiled=True).reshape(1, own, features)

    packed = attention(q_all, kv_all, scale)
    back = lax.all_to_all(packed, ("y", "c"), split_axis=0, concat_axis=0, tiled=True)
    suffix_out, suffix_log = suffix_part(
        queries[0].reshape(own, groups, heads // groups, width),
        generated_keys[0],
        generated_values[0],
        suffix_lengths[0],
        scale,
    )
    count = own * heads
    partial = back[:, :count].astype(F32)
    logs = jnp.sum(back[:, count : count + 3].astype(F32), axis=1)
    suffix_log = suffix_log.reshape(count)
    highest = jnp.maximum(jnp.max(logs, axis=0), suffix_log)
    weight = jnp.exp(logs - highest)
    suffix_weight = jnp.exp(suffix_log - highest)
    total = jnp.sum(weight, axis=0) + suffix_weight
    summed = jnp.sum(partial * weight[..., None], axis=0) + suffix_out.reshape(count, width) * suffix_weight[:, None]
    attended = (summed / total[:, None]).astype(BF16).reshape(1, own, heads, width)
    return attended, expert_mix


def solution(mesh):
    prompts = mesh.shape["prompt"]
    ctx = mesh.shape["ctx"]
    across = math.isqrt(ctx // 2)
    grid = Mesh(mesh.devices.reshape(prompts, across, across, 2), ("x", "z", "y", "c"))
    lay = ("z", "y", "c")
    placed = (
        P("x", lay, None, None),
        P("x", lay, None, None),
        P("x", lay, None, None),
        P("x", lay, None, None, None),
        P("x", lay, None, None, None),
        P("x", lay),
        P("x", lay, None),
        P(lay, None, None),
        P(lay, None, None),
        P(lay, "x", None),
        P(lay, "x", None),
        P(lay, "x", None),
    )
    return jax.shard_map(
        body,
        mesh=grid,
        in_specs=placed,
        out_specs=(P("x", lay, None, None), P("x", lay, None)),
        check_vma=False,
    )
```

time: 953 us -> 195 us (0.20); the launches traced: 942 us -> 194 us
  blocking collectives: 579 us -> 54.7 us
  matrix products: 109 us -> 0.8 us
  waiting for transfers between devices: 132 us -> 43.4 us
  other arithmetic: 59.4 us -> 14.2 us
  starting transfers between devices: 17.3 us -> 38.7 us
  local copies, waits for them, and re-layouts: 29.5 us -> 16.8 us
  Pallas kernels: 0 us -> 11 us
    pmax x1 -> x0, blocking collectives: 489 us -> none  [body(): lax.pmax(local_peak.astype(jnp.bfloat16), 'ctx').astype(local_peak.dtype)]
    dot_general x68 -> x4, matrix products: 109 us -> 0.8 us  [the longest x1 0.23 us: suffix_part(): jnp.einsum('bgqd,bjgd->bgqj', own_query, keys, preferred_element_type=F32)]
    all_to_all x3 -> x4, waiting for transfers between devices: 128 us -> 21.4 us  [the longest x1 17.7 us: body(): lax.all_to_all(packed, ('y', 'c'), split_axis=0, concat_axis=0, tiled=True)]
    reduce_sum x39 -> x5, other arithmetic: 48.2 us -> 0.7 us  [the longest x1 0.35 us: body(): jnp.sum(partial * weight[..., None], axis=0)]
    all_to_all x2 -> x1, blocking collectives: 79.7 us -> 34.1 us  [body(): lax.all_to_all(sent, ('z', 'y', 'c'), split_axis=0, concat_axis=0, tiled=...]
    ppermute x0 -> x6, waiting for transfers between devices: none -> 21.9 us  [the longest x3 12.2 us: body(): lax.ppermute(parts[s], 'x', [(i, (i + s) % prompts) for i in range(prompt...]
    dynamic_update_slice x64 -> x0, local copies, waits for them, and re-layouts: 21.7 us -> none  [body(): summed, totals = lax.map(shifted, (scores, common_peak))]
    ppermute x0 -> x6, starting transfers between devices: none -> 18.5 us  [the longest x3 9.8 us: body(): lax.ppermute(parts[s], 'x', [(i, (i + s) % prompts) for i in range(prompt...]
  transfers between devices with their start and end apart: 4 -> 11, of which waited for: 3 -> 7; matrix products, arithmetic and copies ran while one was open for 21% -> 13% of each run, Pallas kernels for 0% -> 6%
where the time goes in v1:
time: 195 us; the launch traced here: 194 us
  blocking collectives  54.7 us (28%)
  waiting for transfers between devices  43.4 us (22%)
  starting transfers between devices  38.7 us (20%)
  local copies, waits for them, and re-layouts  16.8 us (9%)
  between operations  14.4 us (7%)
  other arithmetic  14.2 us (7%)
  Pallas kernels  11 us (6%)
    all_to_all x1, blocking collectives, body(): lax.all_to_all(sent, ('z', 'y', 'c'), split_axis=0, concat_axis=0, tiled=...  34.1 us
    all_gather x1, blocking collectives, body(): q_all = lax.all_gather(queries[0], ('y', 'c'), axis=0, tiled=False)  20.7 us
    all_to_all x1, waiting for transfers between devices, body(): lax.all_to_all(packed, ('y', 'c'), split_axis=0, concat_axis=0, tiled=True)  17.7 us
    ppermute x3, waiting for transfers between devices, body(): lax.ppermute(parts[s], 'x', [(i, (i + s) % prompts) for i in range(prompt...  12.2 us
    unnamed x1, other arithmetic  11.5 us
    ppermute x3, starting transfers between devices, body(): lax.ppermute(parts[s], 'x', [(i, (i + s) % prompts) for i in range(prompt...  9.8 us
    ppermute x3, waiting for transfers between devices, body(): lax.ppermute(piece, 'x', [(i, (i + s) % prompts) for i in range(prompts)])  9.78 us
    pallas_call x1, Pallas kernels, attention(): pl.pallas_call(lambda *refs: attention_kernel(scale, *refs), grid=(steps,...  9.13 us
  transfers between devices with their start and end apart: 11, of which 7 were waited for; matrix products, arithmetic and copies ran while one was open for 13% of the time, Pallas kernels for 6%

profile of v1, /device:TPU:1, one launch (start us, length us, event | category | flops | bytes accessed | tf_op | source)
XLA Modules:
  0.0 194.0 jit_solution(6848407619765449089)
XLA Ops:
  7.2 1.0 copy_bitcast_fusion
  8.2 0.7 pad_maximum_fusion
  9.0 2.0 %copy.75 = bf16[4,1,2048]{0,1,2:T(2,128)(2,1)S(1)} copy(bf16[4,1,2048]{2,0,1:T(4,128)(2,1)} %bitcast.62) | data formatting | bytes 32768 | tf_op jit(solution)/shard_map/reshape | solution.py:163
  11.5 11.5 %reduce = bf16[2048,4]{1,0:T(8,128)(2,1)S(1)} reduce(bf16[2048,1,4]{2,1,0:T(2,128)(2,1)S(1)} %bitcast.48, bf16[]{:T(256)} %broadcast.43), dimensions={1}, to_apply=%bitcast.34.reduce_sub_computation | reduce | bytes 32770
  23.1 1.4 reshape.204
  24.5 4.8 %all-to-all-start.1 = ((bf16[4,2,1024]{2,1,0:T(2,128)(2,1)}), bf16[4,2,1024]{2,1,0:T(2,128)(2,1)S(1)}, u32[]{:S(2)}, u32[]{:S(2)}) async-start(bf16[4,2,1024]{2,1,0:T(2,128)(2,1)} %reshape.204), calls=%async_computation.1 | async-start | bytes 32768 | tf_op jit(solution)/shard_map/all_to_all | solution.py:162
  29.9 3.7 %all-to-all-done.1 = bf16[4,2,1024]{2,1,0:T(2,128)(2,1)S(1)} async-done(((bf16[4,2,1024]{2,1,0:T(2,128)(2,1)}), bf16[4,2,1024]{2,1,0:T(2,128)(2,1)S(1)}, u32[]{:S(2)}, u32[]{:S(2)}) %all-to-all-start.1) | async-done | bytes 16416 | tf_op jit(solution)/shard_map/all_to_all | solution.py:162
  33.5 2.4 %reshape.205 = bf16[2048,1,4]{2,1,0:T(2,128)(2,1)} reshape(bf16[4,2,1024]{2,1,0:T(2,128)(2,1)S(1)} %all-to-all-done.1) | data formatting | bytes 32768
  36.0 2.3 %copy.76 = bf16[4,1,2048]{2,0,1:T(4,128)(2,1)S(1)} copy(bf16[4,1,2048]{0,1,2:T(2,128)(2,1)} %bitcast.49) | data formatting | bytes 32768 | tf_op jit(solution)/shard_map/all_to_all | solution.py:162
  38.8 34.1 %all_to_all.33 = bf16[128,2,512]{2,1,0:T(2,128)(2,1)S(1)} all-to-all(bf16[128,2,512]{2,1,0:T(2,128)(2,1)S(1)} %copy.78), channel_id=1, replica_groups=mesh['x'=4,'z'=8,'y'=8,'c'=2] {'z','y','c'}, dimensions={0} | all-to-all | bytes 524288 | tf_op jit(solution)/shard_map/all_to_all | solution.py:177
  73.0 2.2 %collective-permute-start = (bf16[256,512]{1,0:T(8,128)(2,1)S(1)}, bf16[256,512]{1,0:T(8,128)(2,1)S(1)}, u32[]{:S(2)}, u32[]{:S(2)}) collective-permute-start(bf16[256,512]{1,0:T(8,128)(2,1)S(1)} %reshape.196.piece0), channel_id=1, source_target_pairs={{0,128},{128,256},{256,384},{384,0},{1,129},{129,257},{257,385},{3... | collective-permute-start | bytes 786440 | tf_op jit(solution)/shard_map/ppermute | solution.py:180
  75.2 3.7 %collective-permute-start.1 = (bf16[256,512]{1,0:T(8,128)(2,1)S(1)}, bf16[256,512]{1,0:T(8,128)(2,1)S(1)}, u32[]{:S(2)}, u32[]{:S(2)}) collective-permute-start(bf16[256,512]{1,0:T(8,128)(2,1)S(1)} %reshape.196.piece0), channel_id=1, source_target_pairs={{0,256},{128,384},{256,0},{384,128},{1,257},{129,385},{257,1},{385... | collective-permute-start | bytes 786440 | tf_op jit(solution)/shard_map/ppermute | solution.py:180
  78.9 2.8 %collective-permute-start.2 = (bf16[256,512]{1,0:T(8,128)(2,1)S(1)}, bf16[256,512]{1,0:T(8,128)(2,1)S(1)}, u32[]{:S(2)}, u32[]{:S(2)}) collective-permute-start(bf16[256,512]{1,0:T(8,128)(2,1)S(1)} %reshape.196.piece0), channel_id=1, source_target_pairs={{0,384},{128,0},{256,128},{384,256},{1,385},{129,1},{257,129},{385... | collective-permute-start | bytes 786440 | tf_op jit(solution)/shard_map/ppermute | solution.py:180
  81.7 2.5 %collective-permute-done.piece1 = bf16[256,512]{1,0:T(8,128)(2,1)S(1)} collective-permute-done((bf16[256,512]{1,0:T(8,128)(2,1)S(1)}, bf16[256,512]{1,0:T(8,128)(2,1)S(1)}, u32[]{:S(2)}, u32[]{:S(2)}) %collective-permute-start) | collective-permute-done | bytes 262176 | tf_op jit(solution)/shard_map/ppermute | solution.py:180
  84.2 4.5 %collective-permute-done.1.piece2 = bf16[256,512]{1,0:T(8,128)(2,1)S(1)} collective-permute-done((bf16[256,512]{1,0:T(8,128)(2,1)S(1)}, bf16[256,512]{1,0:T(8,128)(2,1)S(1)}, u32[]{:S(2)}, u32[]{:S(2)}) %collective-permute-start.1) | collective-permute-done | bytes 262176 | tf_op jit(solution)/shard_map/ppermute | solution.py:180
  88.7 2.8 %collective-permute-done.2.piece3 = bf16[256,512]{1,0:T(8,128)(2,1)S(1)} collective-permute-done((bf16[256,512]{1,0:T(8,128)(2,1)S(1)}, bf16[256,512]{1,0:T(8,128)(2,1)S(1)}, u32[]{:S(2)}, u32[]{:S(2)}) %collective-permute-start.2) | collective-permute-done | bytes 262176 | tf_op jit(solution)/shard_map/ppermute | solution.py:180
  92.2 0.9 copy-done.5
  93.1 1.9 expert_parts.1
  95.0 5.4 %collective-permute-start.5 = (bf16[256,512]{1,0:T(8,128)(2,1)}, bf16[256,512]{1,0:T(8,128)(2,1)S(1)}, u32[]{:S(2)}, u32[]{:S(2)}) collective-permute-start(bf16[256,512]{1,0:T(8,128)(2,1)} %get-tuple-element.9), channel_id=1, source_target_pairs={{0,384},{128,0},{256,128},{384,256},{1,385},{129,1},{257,129},{385... | collective-permute-start | bytes 786440 | tf_op jit(solution)/shard_map/ppermute | solution.py:186
  100.4 1.9 collective-permute-start.4
  102.3 2.5 %collective-permute-start.3 = (bf16[256,512]{1,0:T(8,128)(2,1)}, bf16[256,512]{1,0:T(8,128)(2,1)S(1)}, u32[]{:S(2)}, u32[]{:S(2)}) collective-permute-start(bf16[256,512]{1,0:T(8,128)(2,1)} %get-tuple-element.7), channel_id=1, source_target_pairs={{0,128},{128,256},{256,384},{384,0},{1,129},{129,257},{257,385},{3... | collective-permute-start | bytes 786440 | tf_op jit(solution)/shard_map/ppermute | solution.py:186
  105.7 5.6 %collective-permute-done.5 = bf16[256,512]{1,0:T(8,128)(2,1)S(1)} collective-permute-done((bf16[256,512]{1,0:T(8,128)(2,1)}, bf16[256,512]{1,0:T(8,128)(2,1)S(1)}, u32[]{:S(2)}, u32[]{:S(2)}) %collective-permute-start.5) | collective-permute-done | bytes 262176 | tf_op jit(solution)/shard_map/ppermute | solution.py:186
  111.3 6.5 %collective-permute-done.3 = bf16[256,512]{1,0:T(8,128)(2,1)S(1)} collective-permute-done((bf16[256,512]{1,0:T(8,128)(2,1)}, bf16[256,512]{1,0:T(8,128)(2,1)S(1)}, u32[]{:S(2)}, u32[]{:S(2)}) %collective-permute-start.3) | collective-permute-done | bytes 262176 | tf_op jit(solution)/shard_map/ppermute | solution.py:186
  118.0 0.8 reshape.197
  118.8 5.8 %all-to-all-start.3 = ((bf16[128,2,512]{2,1,0:T(2,128)(2,1)}), bf16[128,2,512]{2,1,0:T(2,128)(2,1)S(1)}, u32[]{:S(2)}, u32[]{:S(2)}) async-start(bf16[128,2,512]{2,1,0:T(2,128)(2,1)} %reshape.197), calls=%async_computation.3 | async-start | bytes 524288 | tf_op jit(solution)/shard_map/all_to_all | solution.py:189
  124.7 20.7 %all_gather.9 = bf16[16,4,32,128]{3,2,1,0:T(8,128)(2,1)S(1)} all-gather(bf16[1,4,32,128]{3,2,1,0:T(8,128)(2,1)S(1)} %copy-done.7), channel_id=1, replica_groups=mesh['x'=4,'z'=8,'y'=8,'c'=2] {'y','c'}, dimensions={0}, use_global_device_ids=true | all-gather | bytes 557056 | tf_op jit(solution)/shard_map/all_gather | solution.py:158
  146.3 3.3 %all-to-all-start.4 = ((bf16[4,4,512]{2,0,1:T(4,128)(2,1)}), bf16[4,4,512]{2,0,1:T(4,128)(2,1)S(1)}, u32[]{:S(2)}, u32[]{:S(2)}) async-start(bf16[4,4,512]{2,0,1:T(4,128)(2,1)} %copy.79), calls=%async_computation.4 | async-start | bytes 32768 | tf_op jit(solution)/shard_map/all_to_all | solution.py:197
  149.6 1.6 copy-done.6
  151.1 9.1 %prompt_attention.1 = bf16[16,144,128]{2,1,0:T(8,128)(2,1)} custom-call(bf16[64,2,16,128]{3,2,1,0:T(8,128)(2,1)S(1)} %bitcast.46, bf16[8,2,2,256,128]{4,3,2,1,0:T(8,128)(2,1)S(1)} %bitcast.47), custom_call_target="tpu_custom_call" | custom-call | flops 3221225472 | bytes 3145728 | tf_op jit(solution)/shard_map/prompt_attention/pallas_call | solution.py:68
  160.3 6.2 %all-to-all-start = ((bf16[16,144,128]{2,1,0:T(8,128)(2,1)}), bf16[16,144,128]{2,1,0:T(8,128)(2,1)S(1)}, u32[]{:S(2)}, u32[]{:S(2)}) async-start(bf16[16,144,128]{2,1,0:T(8,128)(2,1)} %prompt_attention.1), calls=%async_computation | async-start | bytes 1179648 | tf_op jit(solution)/shard_map/all_to_all | solution.py:200
  167.4 17.7 %all-to-all-done = bf16[16,144,128]{2,1,0:T(8,128)(2,1)S(1)} async-done(((bf16[16,144,128]{2,1,0:T(8,128)(2,1)}), bf16[16,144,128]{2,1,0:T(8,128)(2,1)S(1)}, u32[]{:S(2)}, u32[]{:S(2)}) %all-to-all-start) | async-done | bytes 589856 | tf_op jit(solution)/shard_map/all_to_all | solution.py:200
  185.8 0.7 divide_convert_fusion
  (77 shorter events, 6.4 us)
Async XLA Ops:
  7.2 160.0 %copy-start = (bf16[1,4,32,2,128]{4,3,2,1,0:T(2,128)(2,1)S(1)}, bf16[1,4,32,2,128]{4,3,2,1,0:T(2,128)(2,1)}, u32[]{:S(2)}) copy-start(bf16[1,4,32,2,128]{4,3,2,1,0:T(2,128)(2,1)} %param.16) | copy-start | bytes 196612
  7.2 142.4 %all-gather.3.cloned.1.call-start = ((), (), s32[]{:S(2)}) async-start(), calls=%async_computation.5 | async-start | bytes 2359296 | tf_op jit(solution)/shard_map/all_gather | solution.py:157
  8.2 21.1 %copy-start.9 = (s32[4,4,8]{2,1,0:T(4,128)S(1)}, s32[4,4,8]{2,1,0:T(4,128)}, u32[]{:S(2)}) copy-start(s32[4,4,8]{2,1,0:T(4,128)} %param.19) | copy-start | bytes 1540
  24.5 9.1 %all-to-all-start.1 = ((bf16[4,2,1024]{2,1,0:T(2,128)(2,1)}), bf16[4,2,1024]{2,1,0:T(2,128)(2,1)S(1)}, u32[]{:S(2)}, u32[]{:S(2)}) async-start(bf16[4,2,1024]{2,1,0:T(2,128)(2,1)} %reshape.204), calls=%async_computation.1 | async-start | bytes 32768 | tf_op jit(solution)/shard_map/all_to_all | solution.py:162
  29.7 62.5 %copy-start.1 = (bf16[1,192,2048]{2,1,0:T(8,128)(2,1)S(1)}, bf16[1,192,2048]{2,1,0:T(8,128)(2,1)}, u32[]{:S(2)}) copy-start(bf16[1,192,2048]{2,1,0:T(8,128)(2,1)} %param.21) | copy-start | bytes 2359300
  29.7 62.5 %copy-start.2 = (bf16[1,192,2048]{2,1,0:T(8,128)(2,1)S(1)}, bf16[1,192,2048]{2,1,0:T(8,128)(2,1)}, u32[]{:S(2)}) copy-start(bf16[1,192,2048]{2,1,0:T(8,128)(2,1)} %param.22) | copy-start | bytes 2359300
  29.7 62.4 %copy-start.3 = (bf16[1,192,2048]{2,1,0:T(8,128)(2,1)S(1)}, bf16[1,192,2048]{2,1,0:T(8,128)(2,1)}, u32[]{:S(2)}) copy-start(bf16[1,192,2048]{2,1,0:T(8,128)(2,1)} %param.23) | copy-start | bytes 2359300
  73.0 11.2 %collective-permute-start = (bf16[256,512]{1,0:T(8,128)(2,1)S(1)}, bf16[256,512]{1,0:T(8,128)(2,1)S(1)}, u32[]{:S(2)}, u32[]{:S(2)}) collective-permute-start(bf16[256,512]{1,0:T(8,128)(2,1)S(1)} %reshape.196.piece0), channel_id=1, source_target_pairs={{0,128},{128,256},{256,384},{384,0},{1,129},{129,257},{257,385},{3... | collective-permute-start | bytes 786440 | tf_op jit(solution)/shard_map/ppermute | solution.py:180
  75.2 13.5 %collective-permute-start.1 = (bf16[256,512]{1,0:T(8,128)(2,1)S(1)}, bf16[256,512]{1,0:T(8,128)(2,1)S(1)}, u32[]{:S(2)}, u32[]{:S(2)}) collective-permute-start(bf16[256,512]{1,0:T(8,128)(2,1)S(1)} %reshape.196.piece0), channel_id=1, source_target_pairs={{0,256},{128,384},{256,0},{384,128},{1,257},{129,385},{257,1},{385... | collective-permute-start | bytes 786440 | tf_op jit(solution)/shard_map/ppermute | solution.py:180
  78.9 12.6 %collective-permute-start.2 = (bf16[256,512]{1,0:T(8,128)(2,1)S(1)}, bf16[256,512]{1,0:T(8,128)(2,1)S(1)}, u32[]{:S(2)}, u32[]{:S(2)}) collective-permute-start(bf16[256,512]{1,0:T(8,128)(2,1)S(1)} %reshape.196.piece0), channel_id=1, source_target_pairs={{0,384},{128,0},{256,128},{384,256},{1,385},{129,1},{257,129},{385... | collective-permute-start | bytes 786440 | tf_op jit(solution)/shard_map/ppermute | solution.py:180
  91.5 0.7 copy-start.4
  92.2 1.0 copy-start.5
  93.1 11.7 %copy-start.10 = (s32[4,4,8]{2,1,0:T(4,128)S(1)}, s32[4,4,8]{2,1,0:T(4,128)}, u32[]{:S(2)}) copy-start(s32[4,4,8]{2,1,0:T(4,128)} %param.19) | copy-start | bytes 1540
  93.1 11.7 %copy-start.11 = (f32[4,4,8]{2,1,0:T(4,128)S(1)}, f32[4,4,8]{2,1,0:T(4,128)}, u32[]{:S(2)}) copy-start(f32[4,4,8]{2,1,0:T(4,128)} %param.20) | copy-start | bytes 1540
  95.0 29.7 %copy-start.7 = (bf16[1,4,32,128]{3,2,1,0:T(8,128)(2,1)S(1)}, bf16[1,4,32,128]{3,2,1,0:T(8,128)(2,1)}, u32[]{:S(2)}) copy-start(bf16[1,4,32,128]{3,2,1,0:T(8,128)(2,1)} %param.12) | copy-start | bytes 98308
  95.0 16.3 %collective-permute-start.5 = (bf16[256,512]{1,0:T(8,128)(2,1)}, bf16[256,512]{1,0:T(8,128)(2,1)S(1)}, u32[]{:S(2)}, u32[]{:S(2)}) collective-permute-start(bf16[256,512]{1,0:T(8,128)(2,1)} %get-tuple-element.9), channel_id=1, source_target_pairs={{0,384},{128,0},{256,128},{384,256},{1,385},{129,1},{257,129},{385... | collective-permute-start | bytes 786440 | tf_op jit(solution)/shard_map/ppermute | solution.py:186
  100.4 10.9 %collective-permute-start.4 = (bf16[256,512]{1,0:T(8,128)(2,1)}, bf16[256,512]{1,0:T(8,128)(2,1)S(1)}, u32[]{:S(2)}, u32[]{:S(2)}) collective-permute-start(bf16[256,512]{1,0:T(8,128)(2,1)} %get-tuple-element.8), channel_id=1, source_target_pairs={{0,256},{128,384},{256,0},{384,128},{1,257},{129,385},{257,1},{385... | collective-permute-start | bytes 786440 | tf_op jit(solution)/shard_map/ppermute | solution.py:186
  102.3 15.5 %collective-permute-start.3 = (bf16[256,512]{1,0:T(8,128)(2,1)}, bf16[256,512]{1,0:T(8,128)(2,1)S(1)}, u32[]{:S(2)}, u32[]{:S(2)}) collective-permute-start(bf16[256,512]{1,0:T(8,128)(2,1)} %get-tuple-element.7), channel_id=1, source_target_pairs={{0,128},{128,256},{256,384},{384,0},{1,129},{129,257},{257,385},{3... | collective-permute-start | bytes 786440 | tf_op jit(solution)/shard_map/ppermute | solution.py:186
  118.8 26.6 %all-to-all-start.3 = ((bf16[128,2,512]{2,1,0:T(2,128)(2,1)}), bf16[128,2,512]{2,1,0:T(2,128)(2,1)S(1)}, u32[]{:S(2)}, u32[]{:S(2)}) async-start(bf16[128,2,512]{2,1,0:T(2,128)(2,1)} %reshape.197), calls=%async_computation.3 | async-start | bytes 524288 | tf_op jit(solution)/shard_map/all_to_all | solution.py:189
  146.3 14.0 %all-to-all-start.4 = ((bf16[4,4,512]{2,0,1:T(4,128)(2,1)}), bf16[4,4,512]{2,0,1:T(4,128)(2,1)S(1)}, u32[]{:S(2)}, u32[]{:S(2)}) async-start(bf16[4,4,512]{2,0,1:T(4,128)(2,1)} %copy.79), calls=%async_computation.4 | async-start | bytes 32768 | tf_op jit(solution)/shard_map/all_to_all | solution.py:197
  149.5 1.6 copy-start.6
  151.1 15.4 %copy-start.12 = (s32[1,4]{1,0:T(1,128)S(1)}, s32[1,4]{1,0:T(1,128)}, u32[]{:S(2)}) copy-start(s32[1,4]{1,0:T(1,128)} %param.17) | copy-start | bytes 52
  151.1 15.4 %copy-start.8 = (bf16[1,4,32,2,128]{4,3,2,1,0:T(2,128)(2,1)S(1)}, bf16[1,4,32,2,128]{4,3,2,1,0:T(2,128)(2,1)}, u32[]{:S(2)}) copy-start(bf16[1,4,32,2,128]{4,3,2,1,0:T(2,128)(2,1)} %param.15) | copy-start | bytes 196612
  160.3 24.9 %all-to-all-start = ((bf16[16,144,128]{2,1,0:T(8,128)(2,1)}), bf16[16,144,128]{2,1,0:T(8,128)(2,1)S(1)}, u32[]{:S(2)}, u32[]{:S(2)}) async-start(bf16[16,144,128]{2,1,0:T(8,128)(2,1)} %prompt_attention.1), calls=%async_computation | async-start | bytes 1179648 | tf_op jit(solution)/shard_map/all_to_all | solution.py:200
Sparse Core Ops, SparseCore 0:
  10.1 46.2 all-gather.2

commit v2 on v1

v2 whole, which is shorter than its diff:
```python
import functools
import math

import jax
import jax.numpy as jnp
from jax import lax
from jax.experimental import pallas as pl
from jax.experimental.pallas import tpu as pltpu
from jax.sharding import Mesh
from jax.sharding import PartitionSpec as P

BF16 = jnp.bfloat16
F32 = jnp.float32
LOG2E = 1.4426950408889634
NEAR = 4
SLOTS = 2
EXTRA = 16


def three_parts(value):
    high = value.astype(BF16)
    rest = value - high.astype(F32)
    middle = rest.astype(BF16)
    low = (rest - middle.astype(F32)).astype(BF16)
    return high, middle, low


def pack(out_ref, at, values, line):
    rows, width = values.shape
    parts = [part.astype(F32) for part in three_parts(line)]
    extra = jnp.concatenate(parts + [jnp.zeros((EXTRA - 3, width), F32)], axis=0).astype(BF16)
    at = at if isinstance(at, tuple) else (at,)
    out_ref[at + (slice(0, rows),)] = values.astype(BF16)
    out_ref[at + (slice(rows, rows + EXTRA),)] = extra


def unpack_line(ref, at, rows):
    logs = ref[at, rows:, :].astype(F32)
    return logs[0:1] + logs[1:2] + logs[2:3]


def attention_kernel(scale, *refs):
    q_refs, kv_ref, out_refs = refs[:NEAR], refs[NEAR], refs[NEAR + 1 : 2 * NEAR + 1]
    q_buf, k_buf, v_buf, vaug, out_buf, q_sem, kv_sem, out_sem = refs[2 * NEAR + 1 :]
    samples, groups, per_group, width = q_refs[0].shape
    dests = out_refs[0].shape[0]
    own = samples // dests
    positions = kv_ref.shape[0] * kv_ref.shape[3]
    q_in = [pltpu.make_async_copy(q_refs[i], q_buf.at[i], q_sem.at[i]) for i in range(NEAR)]
    k_in = [pltpu.make_async_copy(kv_ref.at[:, 0, g], k_buf.at[g], kv_sem.at[0, g]) for g in range(groups)]
    v_in = [pltpu.make_async_copy(kv_ref.at[:, 1, g], v_buf.at[g], kv_sem.at[1, g]) for g in range(groups)]
    out = [pltpu.make_async_copy(out_buf.at[i], out_refs[i], out_sem.at[i]) for i in range(NEAR)]
    for copy in q_in + k_in + v_in:
        copy.start()
    for g in range(groups):
        vaug[g, :, width:] = jnp.ones((positions, width), BF16)
    for copy in q_in + k_in + v_in:
        copy.wait()
    for g in range(groups):
        vaug[g, :, :width] = v_buf[g].reshape(positions, width)
    for first in (2, 0):
        outs, logs = [], []
        for g in range(groups):
            rows = jnp.concatenate(
                [q_buf[first + i, :, g].reshape(samples * per_group, width) for i in range(2)], axis=0
            )
            keys = k_buf[g].reshape(positions, width)
            scores = lax.dot_general(rows, keys, (((1,), (1,)), ((), ())), preferred_element_type=F32)
            peak = jnp.max(scores, axis=1, keepdims=True)
            probs = jnp.exp2((scores - peak) * (scale * LOG2E)).astype(BF16)
            summed = jnp.dot(probs, vaug[g], preferred_element_type=F32)
            total = summed[:, width:]
            outs.append((summed[:, :width] / total).reshape(2 * samples, 1, per_group, width))
            logs.append((peak * scale + jnp.log(total)).reshape(2 * samples, 1, per_group, width))
        shape = (2 * dests, own * groups * per_group, width)
        values = jnp.concatenate(outs, axis=1).reshape(shape)
        joined = jnp.concatenate(logs, axis=1).reshape(shape)
        for i in range(2):
            for d in range(dests):
                at = i * dests + d
                pack(out_buf, (first + i, d), values[at], jnp.transpose(joined[at])[0:1, :])
    for copy in out:
        copy.start()
    for copy in out:
        copy.wait()


def attention(q_parts, kv_all, scale):
    sources, own, heads, width = q_parts[0].shape
    groups = kv_all.shape[2]
    samples = sources * own
    positions = kv_all.shape[0] * kv_all.shape[3]
    pairs = NEAR * samples * heads * positions
    views = [q.reshape(samples, groups, heads // groups, width) for q in q_parts]
    part = jax.ShapeDtypeStruct((sources, own * heads + EXTRA, width), BF16)
    hbm = pl.BlockSpec(memory_space=pltpu.HBM)
    return pl.pallas_call(
        lambda *refs: attention_kernel(scale, *refs),
        in_specs=[hbm] * (NEAR + 1),
        out_specs=[hbm] * NEAR,
        out_shape=[part] * NEAR,
        scratch_shapes=[
            pltpu.VMEM((NEAR,) + views[0].shape, BF16),
            pltpu.VMEM((groups, kv_all.shape[0], kv_all.shape[3], width), BF16),
            pltpu.VMEM((groups, kv_all.shape[0], kv_all.shape[3], width), BF16),
            pltpu.VMEM((groups, positions, 2 * width), BF16),
            pltpu.VMEM((NEAR,) + part.shape, BF16),
            pltpu.SemaphoreType.DMA((NEAR,)),
            pltpu.SemaphoreType.DMA((2, groups)),
            pltpu.SemaphoreType.DMA((NEAR,)),
        ],
        compiler_params=pltpu.CompilerParams(vmem_limit_bytes=62 * 1024 * 1024),
        cost_estimate=pl.CostEstimate(
            flops=6 * pairs * width, bytes_accessed=2 * (kv_all.size + 8 * q_parts[0].size), transcendentals=pairs
        ),
        name="prompt_attention",
    )(*views, kv_all)


def merged(values, lines):
    highest = functools.reduce(jnp.maximum, lines)
    weights = [jnp.exp(line - highest) for line in lines]
    total = sum(weights)
    shape = values[0].shape
    result = sum(v * jnp.transpose(jnp.broadcast_to(w / total, shape)) for v, w in zip(values, weights, strict=True))
    return result, highest + jnp.log(total)


def merge_kernel(*refs):
    part_refs, keep_ref, send_ref = refs[:-2], refs[-2], refs[-1]
    rows = keep_ref.shape[2]
    for d, out_ref in ((1, send_ref), (0, keep_ref)):
        values, line = merged(
            [ref[d, :rows, :].astype(F32) for ref in part_refs], [unpack_line(ref, d, rows) for ref in part_refs]
        )
        pack(out_ref, 0, values, line)


def merge(parts):
    half = jax.ShapeDtypeStruct((parts[0].shape[0] // 2,) + parts[0].shape[1:], BF16)
    vmem = pl.BlockSpec(memory_space=pltpu.VMEM)
    size = parts[0].size
    return pl.pallas_call(
        merge_kernel,
        in_specs=[vmem] * len(parts),
        out_specs=[vmem] * 2,
        out_shape=[half] * 2,
        cost_estimate=pl.CostEstimate(flops=20 * size, bytes_accessed=10 * size, transcendentals=0),
        name="merge_partials",
    )(*parts)


def last_merge_kernel(mine_ref, other_ref, suffix_ref, suffix_log_ref, out_ref):
    rows = out_ref.shape[0]
    refs = (mine_ref, other_ref)
    values, _ = merged(
        [ref[0, :rows, :].astype(F32) for ref in refs] + [suffix_ref[...]],
        [unpack_line(ref, 0, rows) for ref in refs] + [suffix_log_ref[...]],
    )
    out_ref[...] = values.astype(BF16)


def last_merge(mine, other, suffix, suffix_log):
    vmem = pl.BlockSpec(memory_space=pltpu.VMEM)
    return pl.pallas_call(
        last_merge_kernel,
        in_specs=[vmem] * 4,
        out_specs=vmem,
        out_shape=jax.ShapeDtypeStruct(suffix.shape, BF16),
        cost_estimate=pl.CostEstimate(flops=20 * suffix.size, bytes_accessed=16 * suffix.size, transcendentals=0),
        name="last_merge",
    )(mine, other, suffix, suffix_log)


def expert_kernel(rows_ref, gate_ref, up_ref, down_ref, out_ref):
    parts, rows, width = rows_ref.shape
    dims = (((1,), (1,)), ((), ()))
    gate = up = None
    for part in range(parts):
        columns = slice(part * width, (part + 1) * width)
        piece = rows_ref[part]
        more_gate = lax.dot_general(piece, gate_ref[:, columns], dims, preferred_element_type=F32)
        more_up = lax.dot_general(piece, up_ref[:, columns], dims, preferred_element_type=F32)
        gate = more_gate if gate is None else gate + more_gate
        up = more_up if up is None else up + more_up
    act = (gate / (1.0 + jnp.exp(-gate)) * up).astype(BF16)
    for part in range(parts):
        columns = slice(part * width, (part + 1) * width)
        out_ref[part] = jnp.dot(act, down_ref[:, columns], preferred_element_type=F32).astype(BF16)


def expert_parts(pieces, gate_weight, up_weight, down_weight):
    parts, rows, width = pieces.shape
    vmem = pl.BlockSpec(memory_space=pltpu.VMEM)
    return pl.pallas_call(
        expert_kernel,
        in_specs=[vmem] * 4,
        out_specs=vmem,
        out_shape=jax.ShapeDtypeStruct(pieces.shape, BF16),
        compiler_params=pltpu.CompilerParams(vmem_limit_bytes=24 * 1024 * 1024),
        cost_estimate=pl.CostEstimate(
            flops=6 * rows * width * parts * gate_weight.shape[0],
            bytes_accessed=6 * gate_weight.size + 4 * pieces.size,
            transcendentals=rows * gate_weight.shape[0],
        ),
        name="expert_parts",
    )(pieces, gate_weight, up_weight, down_weight)


def local_kernel(
    scale, prompts, groups, lengths_ref, chosen_ref, shares_ref, q_ref, k_ref, v_ref, slot_ref, share_ref, out_ref, line_ref
):
    rows, top = chosen_ref.shape
    columns = slot_ref.shape[1]
    column = lax.broadcasted_iota(jnp.int32, (rows, columns), 1)
    expert, place = column // SLOTS, column % SLOTS
    chosen, shares = chosen_ref[...], shares_ref[...]
    named = jnp.zeros((rows, columns), F32)
    share = jnp.zeros((rows, columns), F32)
    for k in range(top):
        hit = chosen[:, k : k + 1] == expert
        named = jnp.where(hit, 1.0, named)
        share = jnp.where(hit, shares[:, k : k + 1], share)
    here = lax.broadcasted_iota(jnp.int32, (rows, rows), 0)
    there = lax.broadcasted_iota(jnp.int32, (rows, rows), 1)
    before = jnp.where(there < here, 1.0, 0.0).astype(BF16)
    earlier = jnp.dot(before, named.astype(BF16), preferred_element_type=F32)
    taken = (named > 0.5) & (earlier == place.astype(F32))
    own = rows // prompts
    turn = jnp.where(there == (here % own) * prompts + here // own, 1.0, 0.0).astype(BF16)

    def turned(value):
        return jnp.dot(turn, value, preferred_element_type=F32).astype(BF16)

    share = jnp.where(taken, share, 0.0)
    high = share.astype(BF16)
    low = (share - high.astype(F32)).astype(BF16)
    slot_ref[...] = turned(jnp.where(taken, 1.0, 0.0).astype(BF16))
    share_ref[:rows] = turned(high)
    share_ref[rows:] = turned(low)

    count, width = q_ref.shape
    samples = lengths_ref.shape[0]
    trailing = k_ref.shape[0]
    per_sample, per_group = count // samples, count // samples // groups
    longest = trailing // samples // groups
    row = lax.broadcasted_iota(jnp.int32, (count, trailing), 0)
    col = lax.broadcasted_iota(jnp.int32, (count, trailing), 1)
    sample = row // per_sample
    length = jnp.zeros((count, trailing), jnp.int32)
    for b in range(samples):
        length = jnp.where(sample == b, lengths_ref[b], length)
    live = (
        (sample == col // (longest * groups))
        & (row // per_group % groups == col % groups)
        & (col // groups % longest < length)
    )
    scores = lax.dot_general(q_ref[...], k_ref[...], (((1,), (1,)), ((), ())), preferred_element_type=F32) * scale
    scores = jnp.where(live, scores, -1e30)
    peak = jnp.max(scores, axis=1, keepdims=True)
    terms = jnp.where(live, jnp.exp(scores - peak), 0.0)
    total = jnp.sum(terms, axis=1, keepdims=True)
    out_ref[...] = jnp.dot(terms.astype(BF16), v_ref[...], preferred_element_type=F32) / total
    line_ref[...] = jnp.transpose(jnp.broadcast_to(peak + jnp.log(total), (count, width)))[0:1, :]


def local_work(scale, prompts, experts, lengths, routed_experts, routing_weights, queries, keys, values):
    own, heads, width = queries.shape
    groups = keys.shape[2]
    top = routed_experts.shape[2]
    rows = own * prompts
    vmem = pl.BlockSpec(memory_space=pltpu.VMEM)
    return pl.pallas_call(
        functools.partial(local_kernel, scale, prompts, groups),
        in_specs=[pl.BlockSpec(memory_space=pltpu.SMEM)] + [vmem] * 5,
        out_specs=[vmem] * 4,
        out_shape=[
            jax.ShapeDtypeStruct((rows, experts * SLOTS), BF16),
            jax.ShapeDtypeStruct((2 * rows, experts * SLOTS), BF16),
            jax.ShapeDtypeStruct((own * heads, width), F32),
            jax.ShapeDtypeStruct((1, own * heads), F32),
        ],
        cost_estimate=pl.CostEstimate(flops=10**7, bytes_accessed=10**6, transcendentals=10**5),
        name="local_work",
    )(
        lengths,
        routed_experts.reshape(rows, top),
        routing_weights.reshape(rows, top),
        queries.reshape(own * heads, width),
        keys.reshape(-1, width),
        values.reshape(-1, width),
    )


def columns_kernel(in_ref, out_ref):
    parts, _, width = out_ref.shape
    for part in range(parts):
        out_ref[part] = in_ref[:, part * width : (part + 1) * width]


def columns_first(array, parts):
    rows, width = array.shape
    vmem = pl.BlockSpec(memory_space=pltpu.VMEM)
    return pl.pallas_call(
        columns_kernel,
        in_specs=[vmem],
        out_specs=vmem,
        out_shape=jax.ShapeDtypeStruct((parts, rows, width // parts), array.dtype),
        cost_estimate=pl.CostEstimate(flops=0, bytes_accessed=4 * array.size, transcendentals=0),
        name="columns_first",
    )(array)


def swap(array, distance):
    return lax.ppermute(array, "y", [(i, i ^ distance) for i in range(lax.axis_size("y"))])


def everyone(array, axes):
    copies = jnp.broadcast_to(array[None], (lax.axis_size(axes),) + array.shape)
    return lax.all_to_all(copies, axes, split_axis=0, concat_axis=0, tiled=True)


def suffix_part(own_query, keys, values, lengths, scale):
    scores = jnp.einsum("bgqd,bjgd->bgqj", own_query, keys, preferred_element_type=F32) * scale
    live = (jnp.arange(keys.shape[1], dtype=jnp.int32)[None, :] < lengths[:, None])[:, None, None, :]
    scores = jnp.where(live, scores, -1e30)
    peak = jnp.max(scores, axis=3)
    terms = jnp.where(live, jnp.exp(scores - peak[..., None]), 0.0)
    total = jnp.sum(terms, axis=3)
    summed = jnp.einsum("bgqj,bjgd->bgqd", terms.astype(BF16), values, preferred_element_type=F32)
    return summed / total[..., None], peak + jnp.log(total)


def body(
    queries,
    prefix_keys,
    prompt_value_rows,
    generated_keys,
    generated_values,
    suffix_lengths,
    hidden_rows,
    routed_experts,
    routing_weights,
    gate_weight,
    up_weight,
    down_weight,
):
    prompts = lax.axis_size("x")
    own, heads, width = queries.shape[1:]
    scale = width ** (-0.5)

    features = hidden_rows.shape[2]
    quarter = features // prompts
    experts = lax.axis_size(("z", "y", "c")) * gate_weight.shape[0]
    kv = jnp.stack([prefix_keys[0].transpose(1, 0, 2), prompt_value_rows[0].transpose(1, 0, 2)])
    kv, hidden_rows = lax.optimization_barrier((kv, hidden_rows))
    own_columns = columns_first(hidden_rows[0], prompts)
    kv_all = lax.all_gather(kv, ("z", "c"), axis=0, tiled=False)
    q_pair = jnp.concatenate([queries, swap(queries, NEAR)])

    row_quarter = lax.all_to_all(own_columns, "x", split_axis=0, concat_axis=0, tiled=True)
    slot, share, suffix_out, suffix_line = local_work(
        scale,
        prompts,
        experts,
        suffix_lengths[0],
        routed_experts,
        routing_weights,
        queries[0],
        generated_keys[0],
        generated_values[0],
    )
    row_quarter, q_pair, slot, share, suffix_out, suffix_line = lax.optimization_barrier(
        (row_quarter, q_pair, slot, share, suffix_out, suffix_line)
    )
    sent = jnp.einsum(
        "rc,rd->cd", slot, row_quarter.reshape(prompts * own, quarter), preferred_element_type=F32
    ).astype(BF16)
    arrived = lax.all_to_all(sent.reshape(experts, SLOTS, quarter), ("z", "y", "c"), split_axis=0, concat_axis=0, tiled=True)
    q_parts = [q_pair] + [swap(q_pair, i) for i in range(1, NEAR)]
    arrived, q_parts = lax.optimization_barrier((arrived, q_parts))
    pieces = everyone(arrived.reshape(experts * SLOTS, quarter), "x")
    sums = attention(q_parts, kv_all, scale)
    pieces, sums = lax.optimization_barrier((pieces, sums))
    parts = lax.all_to_all(
        expert_parts(pieces, gate_weight[0], up_weight[0], down_weight[0]), "x", split_axis=0, concat_axis=0, tiled=True
    )
    sums = [sums[0]] + [swap(sums[i], i) for i in range(1, NEAR)]
    parts, sums = lax.optimization_barrier((parts, sums))
    expert_sum = jnp.sum(parts.astype(F32), axis=0).astype(BF16)
    returned = lax.all_to_all(
        expert_sum.reshape(experts, SLOTS, quarter), ("z", "y", "c"), split_axis=0, concat_axis=0, tiled=True
    ).reshape(experts * SLOTS, quarter)
    mine, send = merge(sums)
    other = swap(send, NEAR)
    returned, mine, other = lax.optimization_barrier((returned, mine, other))
    mixed = jnp.dot(share, returned, preferred_element_type=F32)
    mixed = (mixed[: prompts * own] + mixed[prompts * own :]).astype(BF16).reshape(prompts, own, quarter)
    mixed = lax.all_to_all(mixed, "x", split_axis=0, concat_axis=0, tiled=True)
    expert_mix = jnp.concatenate([mixed[p] for p in range(prompts)], axis=1)[None]

    attended = last_merge(mine, other, suffix_out, suffix_line).reshape(1, own, heads, width)
    return attended, expert_mix


def solution(mesh):
    prompts = mesh.shape["prompt"]
    ctx = mesh.shape["ctx"]
    across = math.isqrt(ctx // 2)
    grid = Mesh(mesh.devices.reshape(prompts, across, across, 2), ("x", "z", "y", "c"))
    lay = ("z", "y", "c")
    placed = (
        P("x", lay, None, None),
        P("x", lay, None, None),
        P("x", lay, None, None),
        P("x", lay, None, None, None),
        P("x", lay, None, None, None),
        P("x", lay),
        P("x", lay, None),
        P(lay, None, None),
        P(lay, None, None),
        P(lay, "x", None),
        P(lay, "x", None),
        P(lay, "x", None),
    )
    return jax.shard_map(
        body,
        mesh=grid,
        in_specs=placed,
        out_specs=(P("x", lay, None, None), P("x", lay, None)),
        check_vma=False,
    )
```

time: 195 us -> 146 us (0.75)
  blocking collectives: 54.7 us -> 0 us
  starting transfers between devices: 38.7 us -> 75.2 us
  waiting for transfers between devices: 43.4 us -> 27.2 us
  other arithmetic: 14.2 us -> 2.36 us
  local copies, waits for them, and re-layouts: 16.8 us -> 6.9 us
  Pallas kernels: 11 us -> 18.3 us
    all_to_all x1 -> x0, blocking collectives: 34.1 us -> none  [body(): lax.all_to_all(sent, ('z', 'y', 'c'), split_axis=0, concat_axis=0, tiled=...]
    all_to_all x4 -> x6, starting transfers between devices: 20.2 us -> 41.1 us  [the longest x1 14.4 us: body(): lax.all_to_all(sent.reshape(experts, SLOTS, quarter), ('z', 'y', 'c'), sp...]
    all_gather x1 -> x0, blocking collectives: 20.7 us -> none  [body(): q_all = lax.all_gather(queries[0], ('y', 'c'), axis=0, tiled=False)]
    ppermute x6 -> x8, starting transfers between devices: 18.5 us -> 34 us  [swap(): lax.ppermute(array, 'y', [(i, i ^ distance) for i in range(lax.axis_size(...]
    ppermute x6 -> x8, waiting for transfers between devices: 21.9 us -> 7.2 us  [swap(): lax.ppermute(array, 'y', [(i, i ^ distance) for i in range(lax.axis_size(...]
    unnamed x1 -> x0, other arithmetic: 11.5 us -> none
    pallas_call x2 -> x6, Pallas kernels: 11 us -> 18.3 us  [the longest x1 9.45 us: attention(): pl.pallas_call(lambda *refs: attention_kernel(scale, *refs), in_specs=[hb...]
    unnamed x30, local copies, waits for them, and re-layouts: 8.26 us -> 2.32 us
  transfers between devices with their start and end apart: 11 -> 15, of which waited for: 7 -> 10; matrix products, arithmetic and copies ran while one was open for 13% -> 3% of each run, Pallas kernels for 6% -> 11%
where the time goes in v2:
time: 146 us; the launch traced here: 145 us
  starting transfers between devices  75.2 us (52%)
  waiting for transfers between devices  27.2 us (19%)
  Pallas kernels  18.3 us (13%)
  between operations  14.3 us (10%)
  local copies, waits for them, and re-layouts  6.9 us (5%)
  other arithmetic  2.36 us (2%)
    ppermute x8, starting transfers between devices, swap(): lax.ppermute(array, 'y', [(i, i ^ distance) for i in range(lax.axis_size(...  34 us
    all_to_all x1, starting transfers between devices, body(): lax.all_to_all(sent.reshape(experts, SLOTS, quarter), ('z', 'y', 'c'), sp...  14.4 us
    all_to_all x1, starting transfers between devices, body(): lax.all_to_all(expert_sum.reshape(experts, SLOTS, quarter), ('z', 'y', 'c...  12.3 us
    pallas_call x1, Pallas kernels, attention(): pl.pallas_call(lambda *refs: attention_kernel(scale, *refs), in_specs=[hb...  9.45 us
    ppermute x8, waiting for transfers between devices, swap(): lax.ppermute(array, 'y', [(i, i ^ distance) for i in range(lax.axis_size(...  7.2 us
    all_to_all x1, waiting for transfers between devices, body(): lax.all_to_all(expert_sum.reshape(experts, SLOTS, quarter), ('z', 'y', 'c...  6.54 us
    all_to_all x1, starting transfers between devices, body(): lax.all_to_all(own_columns, 'x', split_axis=0, concat_axis=0, tiled=True)  4.01 us
    all_to_all x1, starting transfers between devices, everyone(): return lax.all_to_all(copies, axes, split_axis=0, concat_axis=0, tiled=True)  3.51 us
  transfers between devices with their start and end apart: 15, of which 10 were waited for; matrix products, arithmetic and copies ran while one was open for 3% of the time, Pallas kernels for 11%

profile of v2, /device:TPU:1, one launch (start us, length us, event | category | flops | bytes accessed | tf_op | source)
XLA Modules:
  0.0 145.3 jit_solution(1318934188370220685)
XLA Ops:
  9.0 8.3 %collective-permute-start = (bf16[1,4,32,128]{3,2,1,0:T(8,128)(2,1)}, bf16[1,4,32,128]{3,2,1,0:T(8,128)(2,1)S(1)}, u32[]{:S(2)}, u32[]{:S(2)}) collective-permute-start(bf16[1,4,32,128]{3,2,1,0:T(8,128)(2,1)} %param.12), channel_id=1, source_target_pairs={{0,8},{2,10},{4,12},{6,14},{8,0},{10,2},{12,4},{14,6},{1,9},{3,11}... | collective-permute-start | bytes 98312 | tf_op jit(solution)/shard_map/ppermute | solution.py:315
  17.3 1.3 columns_first.1
  18.6 4.0 %all-to-all-start = ((bf16[4,4,512]{2,1,0:T(4,128)(2,1)}), bf16[4,4,512]{2,1,0:T(4,128)(2,1)S(1)}, u32[]{:S(2)}, u32[]{:S(2)}) async-start(bf16[4,4,512]{2,1,0:T(4,128)(2,1)} %columns_first.1), calls=%async_computation | async-start | bytes 32768 | tf_op jit(solution)/shard_map/all_to_all | solution.py:361
  22.6 2.0 %local_work.1 = (bf16[16,256]{1,0:T(8,128)(2,1)}, bf16[32,256]{1,0:T(8,128)(2,1)}, f32[128,128]{1,0:T(8,128)}, f32[1,128]{1,0:T(1,128)}) custom-call(s32[4]{0:T(128)} %bitcast.57, s32[16,8]{1,0:T(8,128)} %bitcast.55, f32[16,8]{1,0:T(8,128)} %bitcast.56, bf16[128,128]{1,0:T(8,128)(2,1)} %bitcast.46, bf16[256,128]{1,0:T(8,128)(2,1)} %bitcast.50, ...), custom_call_target="tpu_custom_call" | custom-call | flops 10000000 | bytes 1000000 | tf_op jit(solution)/shard_map/local_work/pallas_call | solution.py:273
  25.3 1.5 %all-to-all-done = bf16[4,4,512]{2,1,0:T(4,128)(2,1)S(1)} async-done(((bf16[4,4,512]{2,1,0:T(4,128)(2,1)}), bf16[4,4,512]{2,1,0:T(4,128)(2,1)S(1)}, u32[]{:S(2)}, u32[]{:S(2)}) %all-to-all-start) | async-done | bytes 16416 | tf_op jit(solution)/shard_map/all_to_all | solution.py:361
  28.6 14.4 %all-to-all-start.1 = ((bf16[128,2,512]{2,1,0:T(2,128)(2,1)}), bf16[128,2,512]{2,1,0:T(2,128)(2,1)S(1)}, u32[]{:S(2)}, u32[]{:S(2)}) async-start(bf16[128,2,512]{2,1,0:T(2,128)(2,1)} %reshape.44), calls=%async_computation.1 | async-start | bytes 524288 | tf_op jit(solution)/shard_map/all_to_all | solution.py:379
  43.0 5.1 %collective-permute-start.3 = (bf16[2,4,32,128]{3,2,1,0:T(8,128)(2,1)S(1)}, bf16[2,4,32,128]{3,2,1,0:T(8,128)(2,1)S(1)}, u32[]{:S(2)}, u32[]{:S(2)}) collective-permute-start(bf16[2,4,32,128]{3,2,1,0:T(8,128)(2,1)S(1)} %pad_maximum_fusion.1), channel_id=1, source_target_pairs={{0,6},{2,4},{4,2},{6,0},{8,14},{10,12},{12,10},{14,8},{1,7},{3,5},... | collective-permute-start | bytes 196616 | tf_op jit(solution)/shard_map/ppermute | solution.py:315
  48.1 1.9 %collective-permute-start.2 = (bf16[2,4,32,128]{3,2,1,0:T(8,128)(2,1)S(1)}, bf16[2,4,32,128]{3,2,1,0:T(8,128)(2,1)S(1)}, u32[]{:S(2)}, u32[]{:S(2)}) collective-permute-start(bf16[2,4,32,128]{3,2,1,0:T(8,128)(2,1)S(1)} %pad_maximum_fusion.1), channel_id=1, source_target_pairs={{0,4},{2,6},{4,0},{6,2},{8,12},{10,14},{12,8},{14,10},{1,5},{3,7},... | collective-permute-start | bytes 196616 | tf_op jit(solution)/shard_map/ppermute | solution.py:315
  50.0 2.3 %collective-permute-start.1 = (bf16[2,4,32,128]{3,2,1,0:T(8,128)(2,1)S(1)}, bf16[2,4,32,128]{3,2,1,0:T(8,128)(2,1)S(1)}, u32[]{:S(2)}, u32[]{:S(2)}) collective-permute-start(bf16[2,4,32,128]{3,2,1,0:T(8,128)(2,1)S(1)} %pad_maximum_fusion.1), channel_id=1, source_target_pairs={{0,2},{2,0},{4,6},{6,4},{8,10},{10,8},{12,14},{14,12},{1,3},{3,1},... | collective-permute-start | bytes 196616 | tf_op jit(solution)/shard_map/ppermute | solution.py:315
  52.4 4.3 %collective-permute-done.2 = bf16[2,4,32,128]{3,2,1,0:T(8,128)(2,1)S(1)} collective-permute-done((bf16[2,4,32,128]{3,2,1,0:T(8,128)(2,1)S(1)}, bf16[2,4,32,128]{3,2,1,0:T(8,128)(2,1)S(1)}, u32[]{:S(2)}, u32[]{:S(2)}) %collective-permute-start.2) | collective-permute-done | bytes 65568 | tf_op jit(solution)/shard_map/ppermute | solution.py:315
  56.7 1.9 %all-to-all-done.1 = bf16[128,2,512]{2,1,0:T(2,128)(2,1)S(1)} async-done(((bf16[128,2,512]{2,1,0:T(2,128)(2,1)}), bf16[128,2,512]{2,1,0:T(2,128)(2,1)S(1)}, u32[]{:S(2)}, u32[]{:S(2)}) %all-to-all-start.1) | async-done | bytes 262176 | tf_op jit(solution)/shard_map/all_to_all | solution.py:379
  58.7 1.1 broadcast_in_dim.11
  59.8 3.5 %all-to-all-start.2 = ((bf16[4,256,512]{2,1,0:T(8,128)(2,1)}), bf16[4,256,512]{2,1,0:T(8,128)(2,1)S(1)}, u32[]{:S(2)}, u32[]{:S(2)}) async-start(bf16[4,256,512]{2,1,0:T(8,128)(2,1)} %broadcast_in_dim.11), calls=%async_computation.2 | async-start | bytes 2097152 | tf_op jit(solution)/shard_map/all_to_all | solution.py:320
  63.3 2.8 %all-gather.3.cloned.1.call-done = bf16[32,2,256,128]{3,2,1,0:T(8,128)(2,1)} async-done(((bf16[2,2,256,128]{3,2,1,0:T(8,128)(2,1)}), bf16[32,2,256,128]{3,2,1,0:T(8,128)(2,1)}) %all-gather.3.cloned.1.call-update) | async-done | bytes 4194320 | tf_op jit(solution)/shard_map/all_gather | solution.py:358
  66.1 9.4 %prompt_attention.1 = (bf16[2,144,128]{2,1,0:T(8,128)(2,1)}, bf16[2,144,128]{2,1,0:T(8,128)(2,1)}, bf16[2,144,128]{2,1,0:T(8,128)(2,1)}, bf16[2,144,128]{2,1,0:T(8,128)(2,1)}) custom-call(bf16[8,2,16,128]{3,2,1,0:T(8,128)(2,1)} %bitcast.45, bf16[8,2,16,128]{3,2,1,0:T(8,128)(2,1)} %bitcast.54, bf16[8,2,16,128]{3,2,1,0:T(8,128)(2,1)} %bitcast.53, ...), custom_call_target="tpu_custom_call" | custom-call | flops 3221225472 | bytes 4718592 | tf_op jit(solution)/shard_map/prompt_attention/pallas_call | solution.py:97
  75.6 2.8 %all-to-all-done.2.rows_ref = bf16[4,256,512]{2,1,0:T(8,128)(2,1)S(1)} async-done(((bf16[4,256,512]{2,1,0:T(8,128)(2,1)}), bf16[4,256,512]{2,1,0:T(8,128)(2,1)S(1)}, u32[]{:S(2)}, u32[]{:S(2)}) %all-to-all-start.2) | async-done | bytes 1048608 | tf_op jit(solution)/shard_map/all_to_all | solution.py:320
  78.4 1.1 copy-done.1
  79.5 1.1 copy-done.2
  80.6 2.1 %expert_parts.1 = bf16[4,256,512]{2,1,0:T(8,128)(2,1)} custom-call(bf16[4,256,512]{2,1,0:T(8,128)(2,1)S(1)} %all-to-all-done.2.rows_ref, bf16[192,2048]{1,0:T(8,128)(2,1)S(1)} %bitcast.42, bf16[192,2048]{1,0:T(8,128)(2,1)S(1)} %bitcast.43, bf16[192,2048]{1,0:T(8,128)(2,1)S(1)} %bitcast.44), custom_call_target="tpu_custom_call" | custom-call | flops 603979776 | bytes 4456448 | tf_op jit(solution)/shard_map/expert_parts/pallas_call | solution.py:195
  82.7 3.5 %all-to-all-start.3 = ((bf16[4,256,512]{2,1,0:T(8,128)(2,1)}), bf16[4,256,512]{2,1,0:T(8,128)(2,1)S(1)}, u32[]{:S(2)}, u32[]{:S(2)}) async-start(bf16[4,256,512]{2,1,0:T(8,128)(2,1)} %expert_parts.1), calls=%async_computation.3 | async-start | bytes 2097152 | tf_op jit(solution)/shard_map/all_to_all | solution.py:385
  86.2 1.9 %collective-permute-start.4 = (bf16[2,144,128]{2,1,0:T(8,128)(2,1)S(1)}, bf16[2,144,128]{2,1,0:T(8,128)(2,1)S(1)}, u32[]{:S(2)}, u32[]{:S(2)}) collective-permute-start(bf16[2,144,128]{2,1,0:T(8,128)(2,1)S(1)} %copy-done.11), channel_id=1, source_target_pairs={{0,2},{2,0},{4,6},{6,4},{8,10},{10,8},{12,14},{14,12},{1,3},{3,1},... | collective-permute-start | bytes 221192 | tf_op jit(solution)/shard_map/ppermute | solution.py:315
  88.2 3.0 %collective-permute-start.5 = (bf16[2,144,128]{2,1,0:T(8,128)(2,1)S(1)}, bf16[2,144,128]{2,1,0:T(8,128)(2,1)S(1)}, u32[]{:S(2)}, u32[]{:S(2)}) collective-permute-start(bf16[2,144,128]{2,1,0:T(8,128)(2,1)S(1)} %copy-done.10), channel_id=1, source_target_pairs={{0,4},{2,6},{4,0},{6,2},{8,12},{10,14},{12,8},{14,10},{1,5},{3,7},... | collective-permute-start | bytes 221192 | tf_op jit(solution)/shard_map/ppermute | solution.py:315
  91.2 4.4 %collective-permute-start.6 = (bf16[2,144,128]{2,1,0:T(8,128)(2,1)S(1)}, bf16[2,144,128]{2,1,0:T(8,128)(2,1)S(1)}, u32[]{:S(2)}, u32[]{:S(2)}) collective-permute-start(bf16[2,144,128]{2,1,0:T(8,128)(2,1)S(1)} %copy-done.9), channel_id=1, source_target_pairs={{0,6},{2,4},{4,2},{6,0},{8,14},{10,12},{12,10},{14,8},{1,7},{3,5},... | collective-permute-start | bytes 221192 | tf_op jit(solution)/shard_map/ppermute | solution.py:315
  95.6 2.8 %collective-permute-done.6.refs_3_ = bf16[2,144,128]{2,1,0:T(8,128)(2,1)S(1)} collective-permute-done((bf16[2,144,128]{2,1,0:T(8,128)(2,1)S(1)}, bf16[2,144,128]{2,1,0:T(8,128)(2,1)S(1)}, u32[]{:S(2)}, u32[]{:S(2)}) %collective-permute-start.6) | collective-permute-done | bytes 73760 | tf_op jit(solution)/shard_map/ppermute | solution.py:315
  98.4 2.0 %all-to-all-done.3 = bf16[4,256,512]{2,1,0:T(8,128)(2,1)S(1)} async-done(((bf16[4,256,512]{2,1,0:T(8,128)(2,1)}), bf16[4,256,512]{2,1,0:T(8,128)(2,1)S(1)}, u32[]{:S(2)}, u32[]{:S(2)}) %all-to-all-start.3) | async-done | bytes 1048608 | tf_op jit(solution)/shard_map/all_to_all | solution.py:385
  101.4 12.3 %all-to-all-start.4 = ((bf16[128,2,512]{2,1,0:T(2,128)(2,1)}), bf16[128,2,512]{2,1,0:T(2,128)(2,1)S(1)}, u32[]{:S(2)}, u32[]{:S(2)}) async-start(bf16[128,2,512]{2,1,0:T(2,128)(2,1)} %reshape.49), calls=%async_computation.4 | async-start | bytes 524288 | tf_op jit(solution)/shard_map/all_to_all | solution.py:391
  113.7 1.8 %merge_partials.1 = (bf16[1,144,128]{2,1,0:T(8,128)(2,1)}, bf16[1,144,128]{2,1,0:T(8,128)(2,1)}) custom-call(bf16[2,144,128]{2,1,0:T(8,128)(2,1)} %get-tuple-element.62.refs_0_, bf16[2,144,128]{2,1,0:T(8,128)(2,1)} %copy-done.3, bf16[2,144,128]{2,1,0:T(8,128)(2,1)} %copy-done.4, bf16[2,144,128]{2,1,0:T(8,128)(2,1)} %copy-done.5), custom_call_target="tpu_custom_call" | custom-call | flops 737280 | bytes 368640 | tf_op jit(solution)/shard_map/merge_partials/pallas_call | solution.py:143
  115.6 7.2 %collective-permute-start.7 = (bf16[1,144,128]{2,1,0:T(8,128)(2,1)}, bf16[1,144,128]{2,1,0:T(8,128)(2,1)S(1)}, u32[]{:S(2)}, u32[]{:S(2)}) collective-permute-start(bf16[1,144,128]{2,1,0:T(8,128)(2,1)} %get-tuple-element.67), channel_id=1, source_target_pairs={{0,8},{2,10},{4,12},{6,14},{8,0},{10,2},{12,4},{14,6},{1,9},{3,11}... | collective-permute-start | bytes 110600 | tf_op jit(solution)/shard_map/ppermute | solution.py:315
  122.8 6.5 %all-to-all-done.4 = bf16[128,2,512]{2,1,0:T(2,128)(2,1)S(1)} async-done(((bf16[128,2,512]{2,1,0:T(2,128)(2,1)}), bf16[128,2,512]{2,1,0:T(2,128)(2,1)S(1)}, u32[]{:S(2)}, u32[]{:S(2)}) %all-to-all-start.4) | async-done | bytes 262176 | tf_op jit(solution)/shard_map/all_to_all | solution.py:391
  130.2 3.4 %all-to-all-start.5 = ((bf16[4,4,512]{2,1,0:T(4,128)(2,1)}), bf16[4,4,512]{2,1,0:T(4,128)(2,1)S(1)}, u32[]{:S(2)}, u32[]{:S(2)}) async-start(bf16[4,4,512]{2,1,0:T(4,128)(2,1)} %reshape.52), calls=%async_computation.5 | async-start | bytes 32768 | tf_op jit(solution)/shard_map/all_to_all | solution.py:399
  133.6 1.7 %last_merge.1 = bf16[128,128]{1,0:T(8,128)(2,1)} custom-call(bf16[1,144,128]{2,1,0:T(8,128)(2,1)} %get-tuple-element.68.mine_ref, bf16[1,144,128]{2,1,0:T(8,128)(2,1)} %copy-done.7, f32[128,128]{1,0:T(8,128)} %get-tuple-element.70.suffix_ref, f32[1,128]{1,0:T(1,128)} %get-tuple-element.71.suffix_log_ref), custom_call_target="tpu_custom_call" | custom-call | flops 327680 | bytes 262144 | tf_op jit(solution)/shard_map/last_merge/pallas_call | solution.py:165
  135.3 2.5 %all-to-all-done.5 = bf16[4,4,512]{2,1,0:T(4,128)(2,1)S(1)} async-done(((bf16[4,4,512]{2,1,0:T(4,128)(2,1)}), bf16[4,4,512]{2,1,0:T(4,128)(2,1)S(1)}, u32[]{:S(2)}, u32[]{:S(2)}) %all-to-all-start.5) | async-done | bytes 16416 | tf_op jit(solution)/shard_map/all_to_all | solution.py:399
  (51 shorter events, 7.1 us)
Async XLA Ops:
  7.2 58.9 %all-gather.3.cloned.1.call-start = ((), (), s32[]{:S(2)}) async-start(), calls=%async_computation.6 | async-start | bytes 4456448 | tf_op jit(solution)/shard_map/all_gather | solution.py:358
  9.0 15.6 %collective-permute-start = (bf16[1,4,32,128]{3,2,1,0:T(8,128)(2,1)}, bf16[1,4,32,128]{3,2,1,0:T(8,128)(2,1)S(1)}, u32[]{:S(2)}, u32[]{:S(2)}) collective-permute-start(bf16[1,4,32,128]{3,2,1,0:T(8,128)(2,1)} %param.12), channel_id=1, source_target_pairs={{0,8},{2,10},{4,12},{6,14},{8,0},{10,2},{12,4},{14,6},{1,9},{3,11}... | collective-permute-start | bytes 98312 | tf_op jit(solution)/shard_map/ppermute | solution.py:315
  18.6 8.2 %all-to-all-start = ((bf16[4,4,512]{2,1,0:T(4,128)(2,1)}), bf16[4,4,512]{2,1,0:T(4,128)(2,1)S(1)}, u32[]{:S(2)}, u32[]{:S(2)}) async-start(bf16[4,4,512]{2,1,0:T(4,128)(2,1)} %columns_first.1), calls=%async_computation | async-start | bytes 32768 | tf_op jit(solution)/shard_map/all_to_all | solution.py:361
  25.3 40.8 %copy-start.6 = (bf16[2,4,32,128]{3,2,1,0:T(8,128)(2,1)}, bf16[2,4,32,128]{3,2,1,0:T(8,128)(2,1)S(1)}, u32[]{:S(2)}) copy-start(bf16[2,4,32,128]{3,2,1,0:T(8,128)(2,1)S(1)} %pad_maximum_fusion.1) | copy-start | bytes 196612
  28.6 30.0 %all-to-all-start.1 = ((bf16[128,2,512]{2,1,0:T(2,128)(2,1)}), bf16[128,2,512]{2,1,0:T(2,128)(2,1)S(1)}, u32[]{:S(2)}, u32[]{:S(2)}) async-start(bf16[128,2,512]{2,1,0:T(2,128)(2,1)} %reshape.44), calls=%async_computation.1 | async-start | bytes 524288 | tf_op jit(solution)/shard_map/all_to_all | solution.py:379
  43.0 9.4 %collective-permute-start.3 = (bf16[2,4,32,128]{3,2,1,0:T(8,128)(2,1)S(1)}, bf16[2,4,32,128]{3,2,1,0:T(8,128)(2,1)S(1)}, u32[]{:S(2)}, u32[]{:S(2)}) collective-permute-start(bf16[2,4,32,128]{3,2,1,0:T(8,128)(2,1)S(1)} %pad_maximum_fusion.1), channel_id=1, source_target_pairs={{0,6},{2,4},{4,2},{6,0},{8,14},{10,12},{12,10},{14,8},{1,7},{3,5},... | collective-permute-start | bytes 196616 | tf_op jit(solution)/shard_map/ppermute | solution.py:315
  48.1 8.6 %collective-permute-start.2 = (bf16[2,4,32,128]{3,2,1,0:T(8,128)(2,1)S(1)}, bf16[2,4,32,128]{3,2,1,0:T(8,128)(2,1)S(1)}, u32[]{:S(2)}, u32[]{:S(2)}) collective-permute-start(bf16[2,4,32,128]{3,2,1,0:T(8,128)(2,1)S(1)} %pad_maximum_fusion.1), channel_id=1, source_target_pairs={{0,4},{2,6},{4,0},{6,2},{8,12},{10,14},{12,8},{14,10},{1,5},{3,7},... | collective-permute-start | bytes 196616 | tf_op jit(solution)/shard_map/ppermute | solution.py:315
  50.0 6.7 %collective-permute-start.1 = (bf16[2,4,32,128]{3,2,1,0:T(8,128)(2,1)S(1)}, bf16[2,4,32,128]{3,2,1,0:T(8,128)(2,1)S(1)}, u32[]{:S(2)}, u32[]{:S(2)}) collective-permute-start(bf16[2,4,32,128]{3,2,1,0:T(8,128)(2,1)S(1)} %pad_maximum_fusion.1), channel_id=1, source_target_pairs={{0,2},{2,0},{4,6},{6,4},{8,10},{10,8},{12,14},{14,12},{1,3},{3,1},... | collective-permute-start | bytes 196616 | tf_op jit(solution)/shard_map/ppermute | solution.py:315
  52.4 13.7 %copy-start.12 = (bf16[2,4,32,128]{3,2,1,0:T(8,128)(2,1)}, bf16[2,4,32,128]{3,2,1,0:T(8,128)(2,1)S(1)}, u32[]{:S(2)}) copy-start(bf16[2,4,32,128]{3,2,1,0:T(8,128)(2,1)S(1)} %collective-permute-done.3) | copy-start | bytes 196612
  56.7 9.4 %copy-start.13 = (bf16[2,4,32,128]{3,2,1,0:T(8,128)(2,1)}, bf16[2,4,32,128]{3,2,1,0:T(8,128)(2,1)S(1)}, u32[]{:S(2)}) copy-start(bf16[2,4,32,128]{3,2,1,0:T(8,128)(2,1)S(1)} %collective-permute-done.2) | copy-start | bytes 196612
  56.7 9.4 %copy-start.14 = (bf16[2,4,32,128]{3,2,1,0:T(8,128)(2,1)}, bf16[2,4,32,128]{3,2,1,0:T(8,128)(2,1)S(1)}, u32[]{:S(2)}) copy-start(bf16[2,4,32,128]{3,2,1,0:T(8,128)(2,1)S(1)} %collective-permute-done.1) | copy-start | bytes 196612
  59.8 18.5 %all-to-all-start.2 = ((bf16[4,256,512]{2,1,0:T(8,128)(2,1)}), bf16[4,256,512]{2,1,0:T(8,128)(2,1)S(1)}, u32[]{:S(2)}, u32[]{:S(2)}) async-start(bf16[4,256,512]{2,1,0:T(8,128)(2,1)} %broadcast_in_dim.11), calls=%async_computation.2 | async-start | bytes 2097152 | tf_op jit(solution)/shard_map/all_to_all | solution.py:320
  66.1 12.2 %copy-start = (bf16[1,192,2048]{2,1,0:T(8,128)(2,1)S(1)}, bf16[1,192,2048]{2,1,0:T(8,128)(2,1)}, u32[]{:S(2)}) copy-start(bf16[1,192,2048]{2,1,0:T(8,128)(2,1)} %param.21) | copy-start | bytes 2359300
  78.4 1.1 copy-start.1
  79.5 1.1 copy-start.2
  80.6 5.6 %copy-start.11 = (bf16[2,144,128]{2,1,0:T(8,128)(2,1)S(1)}, bf16[2,144,128]{2,1,0:T(8,128)(2,1)}, u32[]{:S(2)}) copy-start(bf16[2,144,128]{2,1,0:T(8,128)(2,1)} %get-tuple-element.58) | copy-start | bytes 221188
  80.6 7.6 %copy-start.10 = (bf16[2,144,128]{2,1,0:T(8,128)(2,1)S(1)}, bf16[2,144,128]{2,1,0:T(8,128)(2,1)}, u32[]{:S(2)}) copy-start(bf16[2,144,128]{2,1,0:T(8,128)(2,1)} %get-tuple-element.59) | copy-start | bytes 221188
  80.6 10.5 %copy-start.9 = (bf16[2,144,128]{2,1,0:T(8,128)(2,1)S(1)}, bf16[2,144,128]{2,1,0:T(8,128)(2,1)}, u32[]{:S(2)}) copy-start(bf16[2,144,128]{2,1,0:T(8,128)(2,1)} %get-tuple-element.60) | copy-start | bytes 221188
  80.6 48.8 %copy-start.8 = (bf16[32,256]{1,0:T(8,128)(2,1)S(1)}, bf16[32,256]{1,0:T(8,128)(2,1)}, u32[]{:S(2)}) copy-start(bf16[32,256]{1,0:T(8,128)(2,1)} %get-tuple-element.72) | copy-start | bytes 49156
  82.7 17.6 %all-to-all-start.3 = ((bf16[4,256,512]{2,1,0:T(8,128)(2,1)}), bf16[4,256,512]{2,1,0:T(8,128)(2,1)S(1)}, u32[]{:S(2)}, u32[]{:S(2)}) async-start(bf16[4,256,512]{2,1,0:T(8,128)(2,1)} %expert_parts.1), calls=%async_computation.3 | async-start | bytes 2097152 | tf_op jit(solution)/shard_map/all_to_all | solution.py:385
  86.2 9.3 %collective-permute-start.4 = (bf16[2,144,128]{2,1,0:T(8,128)(2,1)S(1)}, bf16[2,144,128]{2,1,0:T(8,128)(2,1)S(1)}, u32[]{:S(2)}, u32[]{:S(2)}) collective-permute-start(bf16[2,144,128]{2,1,0:T(8,128)(2,1)S(1)} %copy-done.11), channel_id=1, source_target_pairs={{0,2},{2,0},{4,6},{6,4},{8,10},{10,8},{12,14},{14,12},{1,3},{3,1},... | collective-permute-start | bytes 221192 | tf_op jit(solution)/shard_map/ppermute | solution.py:315
  88.2 7.4 %collective-permute-start.5 = (bf16[2,144,128]{2,1,0:T(8,128)(2,1)S(1)}, bf16[2,144,128]{2,1,0:T(8,128)(2,1)S(1)}, u32[]{:S(2)}, u32[]{:S(2)}) collective-permute-start(bf16[2,144,128]{2,1,0:T(8,128)(2,1)S(1)} %copy-done.10), channel_id=1, source_target_pairs={{0,4},{2,6},{4,0},{6,2},{8,12},{10,14},{12,8},{14,10},{1,5},{3,7},... | collective-permute-start | bytes 221192 | tf_op jit(solution)/shard_map/ppermute | solution.py:315
  91.2 7.2 %collective-permute-start.6 = (bf16[2,144,128]{2,1,0:T(8,128)(2,1)S(1)}, bf16[2,144,128]{2,1,0:T(8,128)(2,1)S(1)}, u32[]{:S(2)}, u32[]{:S(2)}) collective-permute-start(bf16[2,144,128]{2,1,0:T(8,128)(2,1)S(1)} %copy-done.9), channel_id=1, source_target_pairs={{0,6},{2,4},{4,2},{6,0},{8,14},{10,12},{12,10},{14,8},{1,7},{3,5},... | collective-permute-start | bytes 221192 | tf_op jit(solution)/shard_map/ppermute | solution.py:315
  95.6 18.1 %copy-start.3 = (bf16[2,144,128]{2,1,0:T(8,128)(2,1)}, bf16[2,144,128]{2,1,0:T(8,128)(2,1)S(1)}, u32[]{:S(2)}) copy-start(bf16[2,144,128]{2,1,0:T(8,128)(2,1)S(1)} %collective-permute-done.4.refs_1_) | copy-start | bytes 221188
  95.6 18.1 %copy-start.4 = (bf16[2,144,128]{2,1,0:T(8,128)(2,1)}, bf16[2,144,128]{2,1,0:T(8,128)(2,1)S(1)}, u32[]{:S(2)}) copy-start(bf16[2,144,128]{2,1,0:T(8,128)(2,1)S(1)} %collective-permute-done.5.refs_2_) | copy-start | bytes 221188
  98.4 15.4 %copy-start.5 = (bf16[2,144,128]{2,1,0:T(8,128)(2,1)}, bf16[2,144,128]{2,1,0:T(8,128)(2,1)S(1)}, u32[]{:S(2)}) copy-start(bf16[2,144,128]{2,1,0:T(8,128)(2,1)S(1)} %collective-permute-done.6.refs_3_) | copy-start | bytes 221188
  101.4 27.9 %all-to-all-start.4 = ((bf16[128,2,512]{2,1,0:T(2,128)(2,1)}), bf16[128,2,512]{2,1,0:T(2,128)(2,1)S(1)}, u32[]{:S(2)}, u32[]{:S(2)}) async-start(bf16[128,2,512]{2,1,0:T(2,128)(2,1)} %reshape.49), calls=%async_computation.4 | async-start | bytes 524288 | tf_op jit(solution)/shard_map/all_to_all | solution.py:391
  115.6 13.8 %collective-permute-start.7 = (bf16[1,144,128]{2,1,0:T(8,128)(2,1)}, bf16[1,144,128]{2,1,0:T(8,128)(2,1)S(1)}, u32[]{:S(2)}, u32[]{:S(2)}) collective-permute-start(bf16[1,144,128]{2,1,0:T(8,128)(2,1)} %get-tuple-element.67), channel_id=1, source_target_pairs={{0,8},{2,10},{4,12},{6,14},{8,0},{10,2},{12,4},{14,6},{1,9},{3,11}... | collective-permute-start | bytes 110600 | tf_op jit(solution)/shard_map/ppermute | solution.py:315
  129.4 4.2 %copy-start.7 = (bf16[1,144,128]{2,1,0:T(8,128)(2,1)}, bf16[1,144,128]{2,1,0:T(8,128)(2,1)S(1)}, u32[]{:S(2)}) copy-start(bf16[1,144,128]{2,1,0:T(8,128)(2,1)S(1)} %collective-permute-done.7.other_ref) | copy-start | bytes 110596
  130.2 7.6 %all-to-all-start.5 = ((bf16[4,4,512]{2,1,0:T(4,128)(2,1)}), bf16[4,4,512]{2,1,0:T(4,128)(2,1)S(1)}, u32[]{:S(2)}, u32[]{:S(2)}) async-start(bf16[4,4,512]{2,1,0:T(4,128)(2,1)} %reshape.52), calls=%async_computation.5 | async-start | bytes 32768 | tf_op jit(solution)/shard_map/all_to_all | solution.py:399
Sparse Core Ops, SparseCore 0:
  10.1 55.9 all-gather.2

commit v3 on v2

--- a/solution.py
+++ b/solution.py
@@ -14,6 +14,7 @@
 LOG2E = 1.4426950408889634
 NEAR = 4
 SLOTS = 2
+LANES = 128
 EXTRA = 16
 
 
@@ -40,49 +41,50 @@
 
 
 def attention_kernel(scale, *refs):
-    q_refs, kv_ref, out_refs = refs[:NEAR], refs[NEAR], refs[NEAR + 1 : 2 * NEAR + 1]
-    q_buf, k_buf, v_buf, vaug, out_buf, q_sem, kv_sem, out_sem = refs[2 * NEAR + 1 :]
+    q_refs, kv_ref, out_ref = refs[:NEAR], refs[NEAR], refs[NEAR + 1]
+    q_buf, k_buf, v_buf, vaug, out_buf, q_sem, kv_sem, out_sem = refs[NEAR + 2 :]
     samples, groups, per_group, width = q_refs[0].shape
-    dests = out_refs[0].shape[0]
+    dests = out_ref.shape[0] // NEAR
     own = samples // dests
     positions = kv_ref.shape[0] * kv_ref.shape[3]
     q_in = [pltpu.make_async_copy(q_refs[i], q_buf.at[i], q_sem.at[i]) for i in range(NEAR)]
-    k_in = [pltpu.make_async_copy(kv_ref.at[:, 0, g], k_buf.at[g], kv_sem.at[0, g]) for g in range(groups)]
-    v_in = [pltpu.make_async_copy(kv_ref.at[:, 1, g], v_buf.at[g], kv_sem.at[1, g]) for g in range(groups)]
-    out = [pltpu.make_async_copy(out_buf.at[i], out_refs[i], out_sem.at[i]) for i in range(NEAR)]
-    for copy in q_in + k_in + v_in:
+    kv_in = [
+        [pltpu.make_async_copy(kv_ref.at[:, i, g], buf.at[g], kv_sem.at[i, g]) for i, buf in enumerate((k_buf, v_buf))]
+        for g in range(groups)
+    ]
+    for copy in q_in + kv_in[0] + kv_in[1]:
         copy.start()
     for g in range(groups):
         vaug[g, :, width:] = jnp.ones((positions, width), BF16)
-    for copy in q_in + k_in + v_in:
+    for copy in q_in + kv_in[0] + kv_in[1]:
         copy.wait()
+    outs, logs = {}, {}
     for g in range(groups):
         vaug[g, :, :width] = v_buf[g].reshape(positions, width)
-    for first in (2, 0):
-        outs, logs = [], []
-        for g in range(groups):
+    for g in range(groups):
+        keys = k_buf[g].reshape(positions, width)
+        for first in (0, 2):
             rows = jnp.concatenate(
                 [q_buf[first + i, :, g].reshape(samples * per_group, width) for i in range(2)], axis=0
             )
-            keys = k_buf[g].reshape(positions, width)
             scores = lax.dot_general(rows, keys, (((1,), (1,)), ((), ())), preferred_element_type=F32)
             peak = jnp.max(scores, axis=1, keepdims=True)
             probs = jnp.exp2((scores - peak) * (scale * LOG2E)).astype(BF16)
             summed = jnp.dot(probs, vaug[g], preferred_element_type=F32)
             total = summed[:, width:]
-            outs.append((summed[:, :width] / total).reshape(2 * samples, 1, per_group, width))
-            logs.append((peak * scale + jnp.log(total)).reshape(2 * samples, 1, per_group, width))
-        shape = (2 * dests, own * groups * per_group, width)
-        values = jnp.concatenate(outs, axis=1).reshape(shape)
-        joined = jnp.concatenate(logs, axis=1).reshape(shape)
+            outs[g, first] = (summed[:, :width] / total).reshape(2 * samples, 1, per_group, width)
+            logs[g, first] = (peak * scale + jnp.log(total)).reshape(2 * samples, 1, per_group, width)
+    shape = (2 * dests, own * groups * per_group, width)
+    for first in (0, 2):
+        values = jnp.concatenate([outs[g, first] for g in range(groups)], axis=1).reshape(shape)
+        joined = jnp.concatenate([logs[g, first] for g in range(groups)], axis=1).reshape(shape)
         for i in range(2):
             for d in range(dests):
                 at = i * dests + d
-                pack(out_buf, (first + i, d), values[at], jnp.transpose(joined[at])[0:1, :])
-    for copy in out:
-        copy.start()
-    for copy in out:
-        copy.wait()
+                pack(out_buf, first + i + NEAR * d, values[at], jnp.transpose(joined[at])[0:1, :])
+    out = pltpu.make_async_copy(out_buf, out_ref, out_sem)
+    out.start()
+    out.wait()
 
 
 def attention(q_parts, kv_all, scale):
@@ -92,24 +94,25 @@
     positions = kv_all.shape[0] * kv_all.shape[3]
     pairs = NEAR * samples * heads * positions
     views = [q.reshape(samples, groups, heads // groups, width) for q in q_parts]
-    part = jax.ShapeDtypeStruct((sources, own * heads + EXTRA, width), BF16)
+    sums = jax.ShapeDtypeStruct((NEAR * sources, own * heads + EXTRA, width), BF16)
     hbm = pl.BlockSpec(memory_space=pltpu.HBM)
+    gathered = (groups, kv_all.shape[0], kv_all.shape[3], width)
     return pl.pallas_call(
         lambda *refs: attention_kernel(scale, *refs),
         in_specs=[hbm] * (NEAR + 1),
-        out_specs=[hbm] * NEAR,
-        out_shape=[part] * NEAR,
+        out_specs=hbm,
+        out_shape=sums,
         scratch_shapes=[
             pltpu.VMEM((NEAR,) + views[0].shape, BF16),
-            pltpu.VMEM((groups, kv_all.shape[0], kv_all.shape[3], width), BF16),
-            pltpu.VMEM((groups, kv_all.shape[0], kv_all.shape[3], width), BF16),
+            pltpu.VMEM(gathered, BF16),
+            pltpu.VMEM(gathered, BF16),
             pltpu.VMEM((groups, positions, 2 * width), BF16),
-            pltpu.VMEM((NEAR,) + part.shape, BF16),
+            pltpu.VMEM(sums.shape, BF16),
             pltpu.SemaphoreType.DMA((NEAR,)),
             pltpu.SemaphoreType.DMA((2, groups)),
-            pltpu.SemaphoreType.DMA((NEAR,)),
+            pltpu.SemaphoreType.DMA,
         ],
-        compiler_params=pltpu.CompilerParams(vmem_limit_bytes=62 * 1024 * 1024),
+        compiler_params=pltpu.CompilerParams(vmem_limit_bytes=60 * 1024 * 1024),
         cost_estimate=pl.CostEstimate(
             flops=6 * pairs * width, bytes_accessed=2 * (kv_all.size + 8 * q_parts[0].size), transcendentals=pairs
         ),
@@ -126,53 +129,41 @@
     return result, highest + jnp.log(total)
 
 
-def merge_kernel(*refs):
-    part_refs, keep_ref, send_ref = refs[:-2], refs[-2], refs[-1]
-    rows = keep_ref.shape[2]
-    for d, out_ref in ((1, send_ref), (0, keep_ref)):
-        values, line = merged(
-            [ref[d, :rows, :].astype(F32) for ref in part_refs], [unpack_line(ref, d, rows) for ref in part_refs]
-        )
-        pack(out_ref, 0, values, line)
-
-
-def merge(parts):
-    half = jax.ShapeDtypeStruct((parts[0].shape[0] // 2,) + parts[0].shape[1:], BF16)
+def merge_kernel(place_ref, all_ref, suffix_ref, suffix_log_ref, out_ref, buf, sems):
+    rows = out_ref.shape[0]
+    sources = all_ref.shape[0]
+    copies = [
+        pltpu.make_async_copy(all_ref.at[i, place_ref[0] ^ i], buf.at[i], sems.at[i]) for i in range(sources)
+    ]
+    for copy in copies:
+        copy.start()
+    for copy in copies:
+        copy.wait()
+    values, _ = merged(
+        [buf[i, :rows, :].astype(F32) for i in range(sources)] + [suffix_ref[...]],
+        [unpack_line(buf, i, rows) for i in range(sources)] + [suffix_log_ref[...]],
+    )
+    out_ref[...] = values.astype(BF16)
+
+
+def merge(place, gathered, suffix, suffix_log):
     vmem = pl.BlockSpec(memory_space=pltpu.VMEM)
-    size = parts[0].size
     return pl.pallas_call(
         merge_kernel,
-        in_specs=[vmem] * len(parts),
-        out_specs=[vmem] * 2,
-        out_shape=[half] * 2,
-        cost_estimate=pl.CostEstimate(flops=20 * size, bytes_accessed=10 * size, transcendentals=0),
-        name="merge_partials",
-    )(*parts)
-
-
-def last_merge_kernel(mine_ref, other_ref, suffix_ref, suffix_log_ref, out_ref):
-    rows = out_ref.shape[0]
-    refs = (mine_ref, other_ref)
-    values, _ = merged(
-        [ref[0, :rows, :].astype(F32) for ref in refs] + [suffix_ref[...]],
-        [unpack_line(ref, 0, rows) for ref in refs] + [suffix_log_ref[...]],
-    )
-    out_ref[...] = values.astype(BF16)
-
-
-def last_merge(mine, other, suffix, suffix_log):
-    vmem = pl.BlockSpec(memory_space=pltpu.VMEM)
-    return pl.pallas_call(
-        last_merge_kernel,
-        in_specs=[vmem] * 4,
+        in_specs=[pl.BlockSpec(memory_space=pltpu.SMEM), pl.BlockSpec(memory_space=pltpu.HBM), vmem, vmem],
         out_specs=vmem,
         out_shape=jax.ShapeDtypeStruct(suffix.shape, BF16),
-        cost_estimate=pl.CostEstimate(flops=20 * suffix.size, bytes_accessed=16 * suffix.size, transcendentals=0),
-        name="last_merge",
-    )(mine, other, suffix, suffix_log)
-
-
-def expert_kernel(rows_ref, gate_ref, up_ref, down_ref, out_ref):
+        scratch_shapes=[
+            pltpu.VMEM((gathered.shape[0],) + gathered.shape[2:], BF16),
+            pltpu.SemaphoreType.DMA((gathered.shape[0],)),
+        ],
+        compiler_params=pltpu.CompilerParams(vmem_limit_bytes=62 * 1024 * 1024),
+        cost_estimate=pl.CostEstimate(flops=60 * suffix.size, bytes_accessed=30 * suffix.size, transcendentals=0),
+        name="merge_partials",
+    )(place, gathered, suffix, suffix_log)
+
+
+def act_kernel(rows_ref, gate_ref, up_ref, out_ref):
     parts, rows, width = rows_ref.shape
     dims = (((1,), (1,)), ((), ()))
     gate = up = None
@@ -183,28 +174,70 @@
         more_up = lax.dot_general(piece, up_ref[:, columns], dims, preferred_element_type=F32)
         gate = more_gate if gate is None else gate + more_gate
         up = more_up if up is None else up + more_up
-    act = (gate / (1.0 + jnp.exp(-gate)) * up).astype(BF16)
+    act = gate / (1.0 + jnp.exp(-gate)) * up
+    half, lanes = rows // 2, out_ref.shape[2]
+    head = act[:, :lanes].astype(BF16)
+    tail = jnp.concatenate([act[:half, lanes:], act[half:, lanes:]], axis=1).astype(BF16)
     for part in range(parts):
-        columns = slice(part * width, (part + 1) * width)
-        out_ref[part] = jnp.dot(act, down_ref[:, columns], preferred_element_type=F32).astype(BF16)
-
-
-def expert_parts(pieces, gate_weight, up_weight, down_weight):
+        out_ref[part, :rows, :] = head
+        out_ref[part, rows:, :] = tail
+
+
+def expert_act(pieces, gate_weight, up_weight):
     parts, rows, width = pieces.shape
+    units = gate_weight.shape[0]
     vmem = pl.BlockSpec(memory_space=pltpu.VMEM)
     return pl.pallas_call(
-        expert_kernel,
-        in_specs=[vmem] * 4,
+        act_kernel,
+        in_specs=[vmem] * 3,
         out_specs=vmem,
-        out_shape=jax.ShapeDtypeStruct(pieces.shape, BF16),
+        out_shape=jax.ShapeDtypeStruct((parts, rows * units // LANES, LANES), BF16),
         compiler_params=pltpu.CompilerParams(vmem_limit_bytes=24 * 1024 * 1024),
         cost_estimate=pl.CostEstimate(
-            flops=6 * rows * width * parts * gate_weight.shape[0],
-            bytes_accessed=6 * gate_weight.size + 4 * pieces.size,
-            transcendentals=rows * gate_weight.shape[0],
+            flops=4 * rows * width * parts * units,
+            bytes_accessed=4 * gate_weight.size + 2 * pieces.size,
+            transcendentals=rows * units,
         ),
-        name="expert_parts",
-    )(pieces, gate_weight, up_weight, down_weight)
+        name="expert_act",
+    )(pieces, gate_weight, up_weight)
+
+
+def out_kernel(units, act_ref, down_ref, out_ref):
+    rows, _ = out_ref.shape
+    half, rest = rows // 2, units - LANES
+    total = None
+    for part in range(act_ref.shape[0]):
+        tail = act_ref[part, rows:, :]
+        weight = down_ref[part, LANES:units, :]
+        more = jnp.dot(act_ref[part, :rows, :], down_ref[part, :LANES, :], preferred_element_type=F32)
+        more = more + jnp.concatenate(
+            [
+                jnp.dot(tail[:, :rest], weight, preferred_element_type=F32),
+                jnp.dot(tail[:, rest:], weight, preferred_element_type=F32),
+            ],
+            axis=0,
+        )
+        total = more if total is None else total + more
+    out_ref[...] = total.astype(BF16)
+
+
+def expert_out(acts, downs, units):
+    parts, _, width = downs.shape
+    rows = acts.shape[1] * LANES // units
+    vmem = pl.BlockSpec(memory_space=pltpu.VMEM)
+    return pl.pallas_call(
+        functools.partial(out_kernel, units),
+        in_specs=[vmem] * 2,
+        out_specs=vmem,
+        out_shape=jax.ShapeDtypeStruct((rows, width), BF16),
+        compiler_params=pltpu.CompilerParams(vmem_limit_bytes=24 * 1024 * 1024),
+        cost_estimate=pl.CostEstimate(
+            flops=2 * rows * width * parts * units,
+            bytes_accessed=2 * (downs.size + acts.size),
+            transcendentals=0,
+        ),
+        name="expert_out",
+    )(acts, downs)
 
 
 def local_kernel(
@@ -292,43 +325,36 @@
     )
 
 
-def columns_kernel(in_ref, out_ref):
-    parts, _, width = out_ref.shape
+def columns_kernel(down_ref, rows_ref, out_ref):
+    units, own = down_ref.shape[0], rows_ref.shape[0]
+    parts, lines, width = out_ref.shape
     for part in range(parts):
-        out_ref[part] = in_ref[:, part * width : (part + 1) * width]
-
-
-def columns_first(array, parts):
-    rows, width = array.shape
+        columns = slice(part * width, (part + 1) * width)
+        out_ref[part, :units, :] = down_ref[:, columns]
+        rows = rows_ref[:, columns].astype(F32)
+        blank = jnp.zeros((lines - units - own, width), F32)
+        out_ref[part, units:, :] = jnp.concatenate([rows, blank], axis=0).astype(BF16)
+
+
+def columns_first(down_weight, rows, parts):
+    units, features = down_weight.shape
     vmem = pl.BlockSpec(memory_space=pltpu.VMEM)
     return pl.pallas_call(
         columns_kernel,
-        in_specs=[vmem],
+        in_specs=[vmem] * 2,
         out_specs=vmem,
-        out_shape=jax.ShapeDtypeStruct((parts, rows, width // parts), array.dtype),
-        cost_estimate=pl.CostEstimate(flops=0, bytes_accessed=4 * array.size, transcendentals=0),
+        out_shape=jax.ShapeDtypeStruct((parts, units + 8, features // parts), BF16),
+        cost_estimate=pl.CostEstimate(flops=0, bytes_accessed=4 * down_weight.size, transcendentals=0),
         name="columns_first",
-    )(array)
+    )(down_weight, rows)
 
 
 def swap(array, distance):
     return lax.ppermute(array, "y", [(i, i ^ distance) for i in range(lax.axis_size("y"))])
 
 
-def everyone(array, axes):
-    copies = jnp.broadcast_to(array[None], (lax.axis_size(axes),) + array.shape)
-    return lax.all_to_all(copies, axes, split_axis=0, concat_axis=0, tiled=True)
-
-
-def suffix_part(own_query, keys, values, lengths, scale):
-    scores = jnp.einsum("bgqd,bjgd->bgqj", own_query, keys, preferred_element_type=F32) * scale
-    live = (jnp.arange(keys.shape[1], dtype=jnp.int32)[None, :] < lengths[:, None])[:, None, None, :]
-    scores = jnp.where(live, scores, -1e30)
-    peak = jnp.max(scores, axis=3)
-    terms = jnp.where(live, jnp.exp(scores - peak[..., None]), 0.0)
-    total = jnp.sum(terms, axis=3)
-    summed = jnp.einsum("bgqj,bjgd->bgqd", terms.astype(BF16), values, preferred_element_type=F32)
-    return summed / total[..., None], peak + jnp.log(total)
+def exchange(array, axes):
+    return lax.all_to_all(array, axes, split_axis=0, concat_axis=0, tiled=True)
 
 
 def body(
@@ -354,11 +380,13 @@
     experts = lax.axis_size(("z", "y", "c")) * gate_weight.shape[0]
     kv = jnp.stack([prefix_keys[0].transpose(1, 0, 2), prompt_value_rows[0].transpose(1, 0, 2)])
     kv, hidden_rows = lax.optimization_barrier((kv, hidden_rows))
-    own_columns = columns_first(hidden_rows[0], prompts)
+    own_columns = columns_first(down_weight[0], hidden_rows[0], prompts)
     kv_all = lax.all_gather(kv, ("z", "c"), axis=0, tiled=False)
     q_pair = jnp.concatenate([queries, swap(queries, NEAR)])
 
-    row_quarter = lax.all_to_all(own_columns, "x", split_axis=0, concat_axis=0, tiled=True)
+    units = down_weight.shape[1]
+    downs = exchange(own_columns, "x")
+    row_quarter = downs[:, units : units + own]
     slot, share, suffix_out, suffix_line = local_work(
         scale,
         prompts,
@@ -379,27 +407,22 @@
     arrived = lax.all_to_all(sent.reshape(experts, SLOTS, quarter), ("z", "y", "c"), split_axis=0, concat_axis=0, tiled=True)
     q_parts = [q_pair] + [swap(q_pair, i) for i in range(1, NEAR)]
     arrived, q_parts = lax.optimization_barrier((arrived, q_parts))
-    pieces = everyone(arrived.reshape(experts * SLOTS, quarter), "x")
+    pieces = arrived.reshape(experts * SLOTS, quarter)
+    pieces = exchange(jnp.broadcast_to(pieces[None], (prompts,) + pieces.shape), "x")
     sums = attention(q_parts, kv_all, scale)
     pieces, sums = lax.optimization_barrier((pieces, sums))
-    parts = lax.all_to_all(
-        expert_parts(pieces, gate_weight[0], up_weight[0], down_weight[0]), "x", split_axis=0, concat_axis=0, tiled=True
-    )
-    sums = [sums[0]] + [swap(sums[i], i) for i in range(1, NEAR)]
-    parts, sums = lax.optimization_barrier((parts, sums))
-    expert_sum = jnp.sum(parts.astype(F32), axis=0).astype(BF16)
-    returned = lax.all_to_all(
-        expert_sum.reshape(experts, SLOTS, quarter), ("z", "y", "c"), split_axis=0, concat_axis=0, tiled=True
-    ).reshape(experts * SLOTS, quarter)
-    mine, send = merge(sums)
-    other = swap(send, NEAR)
-    returned, mine, other = lax.optimization_barrier((returned, mine, other))
+    gathered = lax.all_gather(sums, "y", axis=0, tiled=False)
+    acts = exchange(expert_act(pieces, gate_weight[0], up_weight[0]), "x")
+    outcome = expert_out(acts, downs, units).reshape(experts, SLOTS, quarter)
+    returned = exchange(outcome, ("z", "y", "c")).reshape(experts * SLOTS, quarter)
     mixed = jnp.dot(share, returned, preferred_element_type=F32)
     mixed = (mixed[: prompts * own] + mixed[prompts * own :]).astype(BF16).reshape(prompts, own, quarter)
-    mixed = lax.all_to_all(mixed, "x", split_axis=0, concat_axis=0, tiled=True)
+    mixed = exchange(mixed, "x")
+    place = lax.axis_index("y").astype(jnp.int32).reshape(1)
+    attended = merge(place, gathered, suffix_out, suffix_line)
+    mixed, attended = lax.optimization_barrier((mixed, attended))
     expert_mix = jnp.concatenate([mixed[p] for p in range(prompts)], axis=1)[None]
-
-    attended = last_merge(mine, other, suffix_out, suffix_line).reshape(1, own, heads, width)
+    attended = attended.reshape(1, own, heads, width)
     return attended, expert_mix
 
 

time: 146 us -> 141 us (0.966)
  blocking collectives: 0 us -> 39.3 us
  starting transfers between devices: 75.2 us -> 49.5 us
  waiting for transfers between devices: 27.2 us -> 12.7 us
  local copies, waits for them, and re-layouts: 6.9 us -> 3.9 us
    all_to_all x0 -> x2, blocking collectives: none -> 39.3 us  [exchange(): return lax.all_to_all(array, axes, split_axis=0, concat_axis=0, tiled=True)]
    ppermute x8 -> x4, starting transfers between devices: 34 us -> 16.7 us  [swap(): lax.ppermute(array, 'y', [(i, i ^ distance) for i in range(lax.axis_size(...]
    all_to_all x5 -> x3, starting transfers between devices: 26.7 us -> 11.6 us  [exchange(): return lax.all_to_all(array, axes, split_axis=0, concat_axis=0, tiled=True)]
    all_to_all x5 -> x3, waiting for transfers between devices: 15.3 us -> 6.36 us  [exchange(): return lax.all_to_all(array, axes, split_axis=0, concat_axis=0, tiled=True)]
    all_to_all x1, starting transfers between devices: 14.4 us -> 21.1 us  [body(): lax.all_to_all(sent.reshape(experts, SLOTS, quarter), ('z', 'y', 'c'), sp...]
    all_gather x1, waiting for transfers between devices: 2.77 us -> 0.02 us  [body(): kv_all = lax.all_gather(kv, ('z', 'c'), axis=0, tiled=False)]
    unnamed x30 -> x18, local copies, waits for them, and re-layouts: 2.32 us -> 0.05 us
    ppermute x8 -> x4, waiting for transfers between devices: 7.2 us -> 5.09 us  [swap(): lax.ppermute(array, 'y', [(i, i ^ distance) for i in range(lax.axis_size(...]
  transfers between devices with their start and end apart: 15 -> 10, of which waited for: 10 -> 5; matrix products, arithmetic and copies ran while one was open for 3% -> 3% of each run, Pallas kernels for 11% -> 13%
where the time goes in v3:
time: 141 us; the launch traced here: 140 us
  starting transfers between devices  49.5 us (35%)
  blocking collectives  39.3 us (28%)
  Pallas kernels  17.7 us (13%)
  between operations  14.3 us (10%)
  waiting for transfers between devices  12.7 us (9%)
  local copies, waits for them, and re-layouts  3.9 us (3%)
    all_to_all x2, blocking collectives, exchange(): return lax.all_to_all(array, axes, split_axis=0, concat_axis=0, tiled=True)  39.3 us
    all_to_all x1, starting transfers between devices, body(): lax.all_to_all(sent.reshape(experts, SLOTS, quarter), ('z', 'y', 'c'), sp...  21.1 us
    ppermute x4, starting transfers between devices, swap(): lax.ppermute(array, 'y', [(i, i ^ distance) for i in range(lax.axis_size(...  16.7 us
    all_to_all x3, starting transfers between devices, exchange(): return lax.all_to_all(array, axes, split_axis=0, concat_axis=0, tiled=True)  11.6 us
    pallas_call x1, Pallas kernels, attention(): pl.pallas_call(lambda *refs: attention_kernel(scale, *refs), in_specs=[hb...  9.44 us
    all_to_all x3, waiting for transfers between devices, exchange(): return lax.all_to_all(array, axes, split_axis=0, concat_axis=0, tiled=True)  6.36 us
    ppermute x4, waiting for transfers between devices, swap(): lax.ppermute(array, 'y', [(i, i ^ distance) for i in range(lax.axis_size(...  5.09 us
  transfers between devices with their start and end apart: 10, of which 5 were waited for; matrix products, arithmetic and copies ran while one was open for 3% of the time, Pallas kernels for 13%

profile of v3, /device:TPU:1, one launch (start us, length us, event | category | flops | bytes accessed | tf_op | source)
XLA Modules:
  0.0 139.8 jit_solution(15062481917151060769)
XLA Ops:
  7.2 1.0 copy_bitcast_fusion
  8.2 0.7 pad_maximum_fusion
  9.0 2.1 %columns_first.1 = bf16[4,200,512]{2,1,0:T(8,128)(2,1)} custom-call(bf16[192,2048]{1,0:T(8,128)(2,1)} %bitcast.47, bf16[4,2048]{1,0:T(4,128)(2,1)} %bitcast.51), custom_call_target="tpu_custom_call" | custom-call | bytes 1572864 | tf_op jit(solution)/shard_map/columns_first/pallas_call | solution.py:342
  11.1 4.8 %all-to-all-start = ((bf16[4,200,512]{2,1,0:T(8,128)(2,1)}), bf16[4,200,512]{2,1,0:T(8,128)(2,1)S(1)}, u32[]{:S(2)}, u32[]{:S(2)}) async-start(bf16[4,200,512]{2,1,0:T(8,128)(2,1)} %columns_first.1), calls=%async_computation | async-start | bytes 1638400 | tf_op jit(solution)/shard_map/all_to_all | solution.py:357
  15.9 7.4 %collective-permute-start = (bf16[1,4,32,128]{3,2,1,0:T(8,128)(2,1)S(1)}, bf16[1,4,32,128]{3,2,1,0:T(8,128)(2,1)S(1)}, u32[]{:S(2)}, u32[]{:S(2)}) collective-permute-start(bf16[1,4,32,128]{3,2,1,0:T(8,128)(2,1)S(1)} %copy-done.3), channel_id=1, source_target_pairs={{0,8},{2,10},{4,12},{6,14},{8,0},{10,2},{12,4},{14,6},{1,9},{3,11}... | collective-permute-start | bytes 98312 | tf_op jit(solution)/shard_map/ppermute | solution.py:353
  23.4 1.9 %local_work.1 = (bf16[16,256]{1,0:T(8,128)(2,1)}, bf16[32,256]{1,0:T(8,128)(2,1)}, f32[128,128]{1,0:T(8,128)}, f32[1,128]{1,0:T(1,128)}) custom-call(s32[4]{0:T(128)} %bitcast.60, s32[16,8]{1,0:T(8,128)} %bitcast.58, f32[16,8]{1,0:T(8,128)} %bitcast.59, bf16[128,128]{1,0:T(8,128)(2,1)} %bitcast.50, bf16[256,128]{1,0:T(8,128)(2,1)} %bitcast.53, ...), custom_call_target="tpu_custom_call" | custom-call | flops 10000000 | bytes 1000000 | tf_op jit(solution)/shard_map/local_work/pallas_call | solution.py:306
  25.4 0.9 convolution_convert_fusion
  26.4 0.8 reshape.47
  27.2 21.1 %all-to-all-start.1 = ((bf16[128,2,512]{2,1,0:T(2,128)(2,1)}), bf16[128,2,512]{2,1,0:T(2,128)(2,1)S(1)}, u32[]{:S(2)}, u32[]{:S(2)}) async-start(bf16[128,2,512]{2,1,0:T(2,128)(2,1)} %reshape.47), calls=%async_computation.1 | async-start | bytes 524288 | tf_op jit(solution)/shard_map/all_to_all | solution.py:407
  48.2 3.3 %collective-permute-start.1 = (bf16[2,4,32,128]{3,2,1,0:T(8,128)(2,1)S(1)}, bf16[2,4,32,128]{3,2,1,0:T(8,128)(2,1)S(1)}, u32[]{:S(2)}, u32[]{:S(2)}) collective-permute-start(bf16[2,4,32,128]{3,2,1,0:T(8,128)(2,1)S(1)} %pad_maximum_fusion.1), channel_id=1, source_target_pairs={{0,2},{2,0},{4,6},{6,4},{8,10},{10,8},{12,14},{14,12},{1,3},{3,1},... | collective-permute-start | bytes 196616 | tf_op jit(solution)/shard_map/ppermute | solution.py:353
  51.5 4.0 %collective-permute-start.2 = (bf16[2,4,32,128]{3,2,1,0:T(8,128)(2,1)S(1)}, bf16[2,4,32,128]{3,2,1,0:T(8,128)(2,1)S(1)}, u32[]{:S(2)}, u32[]{:S(2)}) collective-permute-start(bf16[2,4,32,128]{3,2,1,0:T(8,128)(2,1)S(1)} %pad_maximum_fusion.1), channel_id=1, source_target_pairs={{0,4},{2,6},{4,0},{6,2},{8,12},{10,14},{12,8},{14,10},{1,5},{3,7},... | collective-permute-start | bytes 196616 | tf_op jit(solution)/shard_map/ppermute | solution.py:353
  55.5 2.0 %collective-permute-start.3 = (bf16[2,4,32,128]{3,2,1,0:T(8,128)(2,1)S(1)}, bf16[2,4,32,128]{3,2,1,0:T(8,128)(2,1)S(1)}, u32[]{:S(2)}, u32[]{:S(2)}) collective-permute-start(bf16[2,4,32,128]{3,2,1,0:T(8,128)(2,1)S(1)} %pad_maximum_fusion.1), channel_id=1, source_target_pairs={{0,6},{2,4},{4,2},{6,0},{8,14},{10,12},{12,10},{14,8},{1,7},{3,5},... | collective-permute-start | bytes 196616 | tf_op jit(solution)/shard_map/ppermute | solution.py:353
  57.6 0.5 collective-permute-done.2
  58.1 4.6 %collective-permute-done.3 = bf16[2,4,32,128]{3,2,1,0:T(8,128)(2,1)S(1)} collective-permute-done((bf16[2,4,32,128]{3,2,1,0:T(8,128)(2,1)S(1)}, bf16[2,4,32,128]{3,2,1,0:T(8,128)(2,1)S(1)}, u32[]{:S(2)}, u32[]{:S(2)}) %collective-permute-start.3) | collective-permute-done | bytes 65568 | tf_op jit(solution)/shard_map/ppermute | solution.py:353
  62.6 1.2 all-to-all-done.1
  63.8 0.1 broadcast_in_dim.10
  63.9 1.1 broadcast_in_dim.11
  65.0 3.5 %all-to-all-start.2 = ((bf16[4,256,512]{2,1,0:T(8,128)(2,1)}), bf16[4,256,512]{2,1,0:T(8,128)(2,1)S(1)}, u32[]{:S(2)}, u32[]{:S(2)}) async-start(bf16[4,256,512]{2,1,0:T(8,128)(2,1)} %broadcast_in_dim.11), calls=%async_computation.2 | async-start | bytes 2097152 | tf_op jit(solution)/shard_map/all_to_all | solution.py:357
  68.7 9.4 %prompt_attention.1 = bf16[8,144,128]{2,1,0:T(8,128)(2,1)} custom-call(bf16[8,2,16,128]{3,2,1,0:T(8,128)(2,1)} %bitcast.48, bf16[8,2,16,128]{3,2,1,0:T(8,128)(2,1)} %bitcast.55, bf16[8,2,16,128]{3,2,1,0:T(8,128)(2,1)} %bitcast.56, bf16[8,2,16,128]{3,2,1,0:T(8,128)(2,1)} %bitcast.57, bf16[16,2,2,256,128]{4,3,2,1,0:T(8,128)(2,1)} %bitcast.52), custom_call_target="tpu_custom_call" | custom-call | flops 3221225472 | bytes 4718592 | tf_op jit(solution)/shard_map/prompt_attention/pallas_call | solution.py:100
  78.1 4.9 %all-to-all-done.2.rows_ref = bf16[4,256,512]{2,1,0:T(8,128)(2,1)S(1)} async-done(((bf16[4,256,512]{2,1,0:T(8,128)(2,1)}), bf16[4,256,512]{2,1,0:T(8,128)(2,1)S(1)}, u32[]{:S(2)}, u32[]{:S(2)}) %all-to-all-start.2) | async-done | bytes 1048608 | tf_op jit(solution)/shard_map/all_to_all | solution.py:357
  83.1 0.8 expert_act.1
  83.9 8.7 %all_to_all.30.act_ref = bf16[4,384,128]{2,1,0:T(8,128)(2,1)S(1)} all-to-all(bf16[4,384,128]{2,1,0:T(8,128)(2,1)S(1)} %expert_act.1), channel_id=1, replica_groups=mesh['x'=4,'z'=8,'y'=8,'c'=2] {'x'}, dimensions={0} | all-to-all | bytes 786432 | tf_op jit(solution)/shard_map/all_to_all | solution.py:357
  92.6 0.7 expert_out.1
  93.3 0.1 reshape.52
  93.4 30.5 %all_to_all.31 = bf16[128,2,512]{2,1,0:T(2,128)(2,1)S(1)} all-to-all(bf16[128,2,512]{2,1,0:T(2,128)(2,1)S(1)} %reshape.52), channel_id=1, replica_groups=mesh['x'=4,'z'=8,'y'=8,'c'=2] {'z','y','c'}, dimensions={0} | all-to-all | bytes 524288 | tf_op jit(solution)/shard_map/all_to_all | solution.py:357
  124.0 0.1 reshape.53
  124.1 0.1 fusion.1
  124.3 0.6 reshape.54
  124.9 3.3 %all-to-all-start.5 = ((bf16[4,4,512]{2,1,0:T(4,128)(2,1)}), bf16[4,4,512]{2,1,0:T(4,128)(2,1)S(1)}, u32[]{:S(2)}, u32[]{:S(2)}) async-start(bf16[4,4,512]{2,1,0:T(4,128)(2,1)} %reshape.54), calls=%async_computation.5 | async-start | bytes 32768 | tf_op jit(solution)/shard_map/all_to_all | solution.py:357
  128.2 2.7 %merge_partials.1 = bf16[128,128]{1,0:T(8,128)(2,1)} custom-call(s32[1]{0:T(128)} %bitcast.21.place_ref, bf16[8,8,144,128]{3,2,1,0:T(8,128)(2,1)} %bitcast.46, f32[128,128]{1,0:T(8,128)} %get-tuple-element.40.suffix_ref, f32[1,128]{1,0:T(1,128)} %get-tuple-element.41.suffix_log_ref), custom_call_target="tpu_custom_call" | custom-call | flops 983040 | bytes 491520 | tf_op jit(solution)/shard_map/merge_partials/pallas_call | solution.py:151
  130.9 1.4 %all-to-all-done.5 = bf16[4,4,512]{2,1,0:T(4,128)(2,1)S(1)} async-done(((bf16[4,4,512]{2,1,0:T(4,128)(2,1)}), bf16[4,4,512]{2,1,0:T(4,128)(2,1)S(1)}, u32[]{:S(2)}, u32[]{:S(2)}) %all-to-all-start.5) | async-done | bytes 16416 | tf_op jit(solution)/shard_map/all_to_all | solution.py:357
  132.3 0.6 maximum_bitcast_fusion
  (32 shorter events, 0.3 us)
Async XLA Ops:
  7.2 8.8 %copy-start.3 = (bf16[1,4,32,128]{3,2,1,0:T(8,128)(2,1)S(1)}, bf16[1,4,32,128]{3,2,1,0:T(8,128)(2,1)}, u32[]{:S(2)}) copy-start(bf16[1,4,32,128]{3,2,1,0:T(8,128)(2,1)} %param.12) | copy-start | bytes 98308
  7.2 18.2 %copy-start.4 = (bf16[1,4,32,128]{3,2,1,0:T(8,128)(2,1)S(1)}, bf16[1,4,32,128]{3,2,1,0:T(8,128)(2,1)}, u32[]{:S(2)}) copy-start(bf16[1,4,32,128]{3,2,1,0:T(8,128)(2,1)} %param.12) | copy-start | bytes 98308
  7.2 61.4 %all-gather.5.cloned.1.call-start = ((), (), s32[]{:S(2)}) async-start(), calls=%async_computation.6 | async-start | bytes 4456448 | tf_op jit(solution)/shard_map/all_gather | solution.py:384
  11.1 14.3 %all-to-all-start = ((bf16[4,200,512]{2,1,0:T(8,128)(2,1)}), bf16[4,200,512]{2,1,0:T(8,128)(2,1)S(1)}, u32[]{:S(2)}, u32[]{:S(2)}) async-start(bf16[4,200,512]{2,1,0:T(8,128)(2,1)} %columns_first.1), calls=%async_computation | async-start | bytes 1638400 | tf_op jit(solution)/shard_map/all_to_all | solution.py:357
  15.9 9.4 %collective-permute-start = (bf16[1,4,32,128]{3,2,1,0:T(8,128)(2,1)S(1)}, bf16[1,4,32,128]{3,2,1,0:T(8,128)(2,1)S(1)}, u32[]{:S(2)}, u32[]{:S(2)}) collective-permute-start(bf16[1,4,32,128]{3,2,1,0:T(8,128)(2,1)S(1)} %copy-done.3), channel_id=1, source_target_pairs={{0,8},{2,10},{4,12},{6,14},{8,0},{10,2},{12,4},{14,6},{1,9},{3,11}... | collective-permute-start | bytes 98312 | tf_op jit(solution)/shard_map/ppermute | solution.py:353
  25.4 43.3 %copy-start.2 = (bf16[2,4,32,128]{3,2,1,0:T(8,128)(2,1)}, bf16[2,4,32,128]{3,2,1,0:T(8,128)(2,1)S(1)}, u32[]{:S(2)}) copy-start(bf16[2,4,32,128]{3,2,1,0:T(8,128)(2,1)S(1)} %pad_maximum_fusion.1) | copy-start | bytes 196612
  27.2 36.6 %all-to-all-start.1 = ((bf16[128,2,512]{2,1,0:T(2,128)(2,1)}), bf16[128,2,512]{2,1,0:T(2,128)(2,1)S(1)}, u32[]{:S(2)}, u32[]{:S(2)}) async-start(bf16[128,2,512]{2,1,0:T(2,128)(2,1)} %reshape.47), calls=%async_computation.1 | async-start | bytes 524288 | tf_op jit(solution)/shard_map/all_to_all | solution.py:407
  48.2 9.3 %collective-permute-start.1 = (bf16[2,4,32,128]{3,2,1,0:T(8,128)(2,1)S(1)}, bf16[2,4,32,128]{3,2,1,0:T(8,128)(2,1)S(1)}, u32[]{:S(2)}, u32[]{:S(2)}) collective-permute-start(bf16[2,4,32,128]{3,2,1,0:T(8,128)(2,1)S(1)} %pad_maximum_fusion.1), channel_id=1, source_target_pairs={{0,2},{2,0},{4,6},{6,4},{8,10},{10,8},{12,14},{14,12},{1,3},{3,1},... | collective-permute-start | bytes 196616 | tf_op jit(solution)/shard_map/ppermute | solution.py:353
  51.5 6.5 %collective-permute-start.2 = (bf16[2,4,32,128]{3,2,1,0:T(8,128)(2,1)S(1)}, bf16[2,4,32,128]{3,2,1,0:T(8,128)(2,1)S(1)}, u32[]{:S(2)}, u32[]{:S(2)}) collective-permute-start(bf16[2,4,32,128]{3,2,1,0:T(8,128)(2,1)S(1)} %pad_maximum_fusion.1), channel_id=1, source_target_pairs={{0,4},{2,6},{4,0},{6,2},{8,12},{10,14},{12,8},{14,10},{1,5},{3,7},... | collective-permute-start | bytes 196616 | tf_op jit(solution)/shard_map/ppermute | solution.py:353
  55.5 7.1 %collective-permute-start.3 = (bf16[2,4,32,128]{3,2,1,0:T(8,128)(2,1)S(1)}, bf16[2,4,32,128]{3,2,1,0:T(8,128)(2,1)S(1)}, u32[]{:S(2)}, u32[]{:S(2)}) collective-permute-start(bf16[2,4,32,128]{3,2,1,0:T(8,128)(2,1)S(1)} %pad_maximum_fusion.1), channel_id=1, source_target_pairs={{0,6},{2,4},{4,2},{6,0},{8,14},{10,12},{12,10},{14,8},{1,7},{3,5},... | collective-permute-start | bytes 196616 | tf_op jit(solution)/shard_map/ppermute | solution.py:353
  57.5 11.1 %copy-start.6 = (bf16[2,4,32,128]{3,2,1,0:T(8,128)(2,1)}, bf16[2,4,32,128]{3,2,1,0:T(8,128)(2,1)S(1)}, u32[]{:S(2)}) copy-start(bf16[2,4,32,128]{3,2,1,0:T(8,128)(2,1)S(1)} %collective-permute-done.1) | copy-start | bytes 196612
  58.1 10.5 %copy-start.7 = (bf16[2,4,32,128]{3,2,1,0:T(8,128)(2,1)}, bf16[2,4,32,128]{3,2,1,0:T(8,128)(2,1)S(1)}, u32[]{:S(2)}) copy-start(bf16[2,4,32,128]{3,2,1,0:T(8,128)(2,1)S(1)} %collective-permute-done.2) | copy-start | bytes 196612
  62.6 6.0 %copy-start.8 = (bf16[2,4,32,128]{3,2,1,0:T(8,128)(2,1)}, bf16[2,4,32,128]{3,2,1,0:T(8,128)(2,1)S(1)}, u32[]{:S(2)}) copy-start(bf16[2,4,32,128]{3,2,1,0:T(8,128)(2,1)S(1)} %collective-permute-done.3) | copy-start | bytes 196612
  65.0 18.0 %all-to-all-start.2 = ((bf16[4,256,512]{2,1,0:T(8,128)(2,1)}), bf16[4,256,512]{2,1,0:T(8,128)(2,1)S(1)}, u32[]{:S(2)}, u32[]{:S(2)}) async-start(bf16[4,256,512]{2,1,0:T(8,128)(2,1)} %broadcast_in_dim.11), calls=%async_computation.2 | async-start | bytes 2097152 | tf_op jit(solution)/shard_map/all_to_all | solution.py:357
  68.5 59.6 %all-gather.7.cloned.1.call-start = ((), (), s32[]{:S(2)}) async-start(), calls=%async_computation.7 | async-start | bytes 2654208 | tf_op jit(solution)/shard_map/all_gather | solution.py:414
  68.6 14.4 %copy-start = (bf16[1,192,2048]{2,1,0:T(8,128)(2,1)S(1)}, bf16[1,192,2048]{2,1,0:T(8,128)(2,1)}, u32[]{:S(2)}) copy-start(bf16[1,192,2048]{2,1,0:T(8,128)(2,1)} %param.21) | copy-start | bytes 2359300
  68.6 14.4 %copy-start.1 = (bf16[1,192,2048]{2,1,0:T(8,128)(2,1)S(1)}, bf16[1,192,2048]{2,1,0:T(8,128)(2,1)}, u32[]{:S(2)}) copy-start(bf16[1,192,2048]{2,1,0:T(8,128)(2,1)} %param.22) | copy-start | bytes 2359300
  78.1 46.0 %copy-start.5 = (bf16[32,256]{1,0:T(8,128)(2,1)S(1)}, bf16[32,256]{1,0:T(8,128)(2,1)}, u32[]{:S(2)}) copy-start(bf16[32,256]{1,0:T(8,128)(2,1)} %get-tuple-element.28) | copy-start | bytes 49156
  124.9 7.4 %all-to-all-start.5 = ((bf16[4,4,512]{2,1,0:T(4,128)(2,1)}), bf16[4,4,512]{2,1,0:T(4,128)(2,1)S(1)}, u32[]{:S(2)}, u32[]{:S(2)}) async-start(bf16[4,4,512]{2,1,0:T(4,128)(2,1)} %reshape.54), calls=%async_computation.5 | async-start | bytes 32768 | tf_op jit(solution)/shard_map/all_to_all | solution.py:357
Sparse Core Ops, SparseCore 0:
  10.1 55.8 all-gather.4
  83.2 43.1 all-gather.6

commit v4 on v3

--- a/solution.py
+++ b/solution.py
@@ -15,7 +15,7 @@
 NEAR = 4
 SLOTS = 2
 LANES = 128
-EXTRA = 16
+TERMS = 3
 
 
 def three_parts(value):
@@ -26,26 +26,12 @@
     return high, middle, low
 
 
-def pack(out_ref, at, values, line):
-    rows, width = values.shape
-    parts = [part.astype(F32) for part in three_parts(line)]
-    extra = jnp.concatenate(parts + [jnp.zeros((EXTRA - 3, width), F32)], axis=0).astype(BF16)
-    at = at if isinstance(at, tuple) else (at,)
-    out_ref[at + (slice(0, rows),)] = values.astype(BF16)
-    out_ref[at + (slice(rows, rows + EXTRA),)] = extra
-
-
-def unpack_line(ref, at, rows):
-    logs = ref[at, rows:, :].astype(F32)
-    return logs[0:1] + logs[1:2] + logs[2:3]
-
-
 def attention_kernel(scale, *refs):
     q_refs, kv_ref, out_ref = refs[:NEAR], refs[NEAR], refs[NEAR + 1]
     q_buf, k_buf, v_buf, vaug, out_buf, q_sem, kv_sem, out_sem = refs[NEAR + 2 :]
     samples, groups, per_group, width = q_refs[0].shape
-    dests = out_ref.shape[0] // NEAR
-    own = samples // dests
+    own = samples * groups * per_group // width
+    dests, own = own, samples // own
     positions = kv_ref.shape[0] * kv_ref.shape[3]
     q_in = [pltpu.make_async_copy(q_refs[i], q_buf.at[i], q_sem.at[i]) for i in range(NEAR)]
     kv_in = [
@@ -58,7 +44,7 @@
         vaug[g, :, width:] = jnp.ones((positions, width), BF16)
     for copy in q_in + kv_in[0] + kv_in[1]:
         copy.wait()
-    outs, logs = {}, {}
+    outs, logs, lines = {}, {}, {}
     for g in range(groups):
         vaug[g, :, :width] = v_buf[g].reshape(positions, width)
     for g in range(groups):
@@ -81,7 +67,13 @@
         for i in range(2):
             for d in range(dests):
                 at = i * dests + d
-                pack(out_buf, first + i + NEAR * d, values[at], jnp.transpose(joined[at])[0:1, :])
+                to = first + i + NEAR * d
+                out_buf[to * width : (to + 1) * width, :] = values[at].astype(BF16)
+                lines[to] = [part.astype(F32) for part in three_parts(jnp.transpose(joined[at])[0:1, :])]
+    used = NEAR * dests * width
+    extra = sum([lines[to] for to in range(NEAR * dests)], [])
+    extra.append(jnp.zeros((out_ref.shape[0] - used - len(extra), width), F32))
+    out_buf[used:, :] = jnp.concatenate(extra, axis=0).astype(BF16)
     out = pltpu.make_async_copy(out_buf, out_ref, out_sem)
     out.start()
     out.wait()
@@ -94,7 +86,8 @@
     positions = kv_all.shape[0] * kv_all.shape[3]
     pairs = NEAR * samples * heads * positions
     views = [q.reshape(samples, groups, heads // groups, width) for q in q_parts]
-    sums = jax.ShapeDtypeStruct((NEAR * sources, own * heads + EXTRA, width), BF16)
+    count = NEAR * sources
+    sums = jax.ShapeDtypeStruct((count * own * heads + -(-count * TERMS // 16) * 16, width), BF16)
     hbm = pl.BlockSpec(memory_space=pltpu.HBM)
     gathered = (groups, kv_all.shape[0], kv_all.shape[3], width)
     return pl.pallas_call(
@@ -129,24 +122,34 @@
     return result, highest + jnp.log(total)
 
 
-def merge_kernel(place_ref, all_ref, suffix_ref, suffix_log_ref, out_ref, buf, sems):
+def merge_kernel(place_ref, all_ref, suffix_ref, suffix_log_ref, out_ref, buf, extra, sems):
     rows = out_ref.shape[0]
-    sources = all_ref.shape[0]
-    copies = [
-        pltpu.make_async_copy(all_ref.at[i, place_ref[0] ^ i], buf.at[i], sems.at[i]) for i in range(sources)
-    ]
+    sources, lines = extra.shape[:2]
+    copies = []
+    for i in range(sources):
+        start = pl.multiple_of((place_ref[0] ^ i) * rows, rows)
+        copies.append(pltpu.make_async_copy(all_ref.at[i, pl.ds(start, rows)], buf.at[i], sems.at[0, i]))
+        copies.append(
+            pltpu.make_async_copy(all_ref.at[i, pl.ds(sources * rows, lines)], extra.at[i], sems.at[1, i])
+        )
     for copy in copies:
         copy.start()
     for copy in copies:
         copy.wait()
+    owner = lax.broadcasted_iota(jnp.int32, extra.shape[1:], 0) // TERMS
+    logs = [
+        jnp.sum(jnp.where(owner == (place_ref[0] ^ i), extra[i].astype(F32), 0.0), axis=0, keepdims=True)
+        for i in range(sources)
+    ]
     values, _ = merged(
-        [buf[i, :rows, :].astype(F32) for i in range(sources)] + [suffix_ref[...]],
-        [unpack_line(buf, i, rows) for i in range(sources)] + [suffix_log_ref[...]],
+        [buf[i].astype(F32) for i in range(sources)] + [suffix_ref[...]], logs + [suffix_log_ref[...]]
     )
     out_ref[...] = values.astype(BF16)
 
 
 def merge(place, gathered, suffix, suffix_log):
+    sources, lines, width = gathered.shape
+    rows = suffix.shape[0]
     vmem = pl.BlockSpec(memory_space=pltpu.VMEM)
     return pl.pallas_call(
         merge_kernel,
@@ -154,8 +157,9 @@
         out_specs=vmem,
         out_shape=jax.ShapeDtypeStruct(suffix.shape, BF16),
         scratch_shapes=[
-            pltpu.VMEM((gathered.shape[0],) + gathered.shape[2:], BF16),
-            pltpu.SemaphoreType.DMA((gathered.shape[0],)),
+            pltpu.VMEM((sources, rows, width), BF16),
+            pltpu.VMEM((sources, lines - sources * rows, width), BF16),
+            pltpu.SemaphoreType.DMA((2, sources)),
         ],
         compiler_params=pltpu.CompilerParams(vmem_limit_bytes=62 * 1024 * 1024),
         cost_estimate=pl.CostEstimate(flops=60 * suffix.size, bytes_accessed=30 * suffix.size, transcendentals=0),
@@ -405,7 +409,7 @@
         "rc,rd->cd", slot, row_quarter.reshape(prompts * own, quarter), preferred_element_type=F32
     ).astype(BF16)
     arrived = lax.all_to_all(sent.reshape(experts, SLOTS, quarter), ("z", "y", "c"), split_axis=0, concat_axis=0, tiled=True)
-    q_parts = [q_pair] + [swap(q_pair, i) for i in range(1, NEAR)]
+    q_parts = ([swap(q_pair, i) for i in range(NEAR - 1, 0, -1)] + [q_pair])[::-1]
     arrived, q_parts = lax.optimization_barrier((arrived, q_parts))
     pieces = arrived.reshape(experts * SLOTS, quarter)
     pieces = exchange(jnp.broadcast_to(pieces[None], (prompts,) + pieces.shape), "x")

time: 141 us -> 141 us (level)
  no operation moved by 1% of the time
where the time goes in v4:
time: 141 us; the launch traced here: 140 us
  starting transfers between devices  49.4 us (35%)
  blocking collectives  39.6 us (28%)
  Pallas kernels  17.8 us (13%)
  between operations  14.3 us (10%)
  waiting for transfers between devices  12.5 us (9%)
  local copies, waits for them, and re-layouts  3.9 us (3%)
    all_to_all x2, blocking collectives, exchange(): return lax.all_to_all(array, axes, split_axis=0, concat_axis=0, tiled=True)  39.6 us
    all_to_all x1, starting transfers between devices, body(): lax.all_to_all(sent.reshape(experts, SLOTS, quarter), ('z', 'y', 'c'), sp...  21 us
    ppermute x4, starting transfers between devices, swap(): lax.ppermute(array, 'y', [(i, i ^ distance) for i in range(lax.axis_size(...  16.7 us
    all_to_all x3, starting transfers between devices, exchange(): return lax.all_to_all(array, axes, split_axis=0, concat_axis=0, tiled=True)  11.6 us
    pallas_call x1, Pallas kernels, attention(): pl.pallas_call(lambda *refs: attention_kernel(scale, *refs), in_specs=[hb...  9.43 us
    all_to_all x3, waiting for transfers between devices, exchange(): return lax.all_to_all(array, axes, split_axis=0, concat_axis=0, tiled=True)  6.23 us
    ppermute x4, waiting for transfers between devices, swap(): lax.ppermute(array, 'y', [(i, i ^ distance) for i in range(lax.axis_size(...  5.09 us
    pallas_call x1, Pallas kernels, merge(): pl.pallas_call(merge_kernel, in_specs=[pl.BlockSpec(memory_space=pltpu.SM...  2.84 us
  transfers between devices with their start and end apart: 10, of which 5 were waited for; matrix products, arithmetic and copies ran while one was open for 3% of the time, Pallas kernels for 13%

profile of v4, /device:TPU:1, one launch (start us, length us, event | category | flops | bytes accessed | tf_op | source)
XLA Modules:
  0.0 140.1 jit_solution(13709049362683026294)
XLA Ops:
  7.2 1.0 copy_bitcast_fusion
  8.2 0.7 pad_maximum_fusion
  9.0 2.1 %columns_first.1 = bf16[4,200,512]{2,1,0:T(8,128)(2,1)} custom-call(bf16[192,2048]{1,0:T(8,128)(2,1)} %bitcast.47, bf16[4,2048]{1,0:T(4,128)(2,1)} %bitcast.51), custom_call_target="tpu_custom_call" | custom-call | bytes 1572864 | tf_op jit(solution)/shard_map/columns_first/pallas_call | solution.py:346
  11.1 4.8 %all-to-all-start = ((bf16[4,200,512]{2,1,0:T(8,128)(2,1)}), bf16[4,200,512]{2,1,0:T(8,128)(2,1)S(1)}, u32[]{:S(2)}, u32[]{:S(2)}) async-start(bf16[4,200,512]{2,1,0:T(8,128)(2,1)} %columns_first.1), calls=%async_computation | async-start | bytes 1638400 | tf_op jit(solution)/shard_map/all_to_all | solution.py:361
  15.9 7.4 %collective-permute-start = (bf16[1,4,32,128]{3,2,1,0:T(8,128)(2,1)S(1)}, bf16[1,4,32,128]{3,2,1,0:T(8,128)(2,1)S(1)}, u32[]{:S(2)}, u32[]{:S(2)}) collective-permute-start(bf16[1,4,32,128]{3,2,1,0:T(8,128)(2,1)S(1)} %copy-done.3), channel_id=1, source_target_pairs={{0,8},{2,10},{4,12},{6,14},{8,0},{10,2},{12,4},{14,6},{1,9},{3,11}... | collective-permute-start | bytes 98312 | tf_op jit(solution)/shard_map/ppermute | solution.py:357
  23.4 2.0 %local_work.1 = (bf16[16,256]{1,0:T(8,128)(2,1)}, bf16[32,256]{1,0:T(8,128)(2,1)}, f32[128,128]{1,0:T(8,128)}, f32[1,128]{1,0:T(1,128)}) custom-call(s32[4]{0:T(128)} %bitcast.60, s32[16,8]{1,0:T(8,128)} %bitcast.58, f32[16,8]{1,0:T(8,128)} %bitcast.59, bf16[128,128]{1,0:T(8,128)(2,1)} %bitcast.50, bf16[256,128]{1,0:T(8,128)(2,1)} %bitcast.53, ...), custom_call_target="tpu_custom_call" | custom-call | flops 10000000 | bytes 1000000 | tf_op jit(solution)/shard_map/local_work/pallas_call | solution.py:310
  25.4 0.9 convolution_convert_fusion
  26.4 0.8 reshape.47
  27.2 21.0 %all-to-all-start.1 = ((bf16[128,2,512]{2,1,0:T(2,128)(2,1)}), bf16[128,2,512]{2,1,0:T(2,128)(2,1)S(1)}, u32[]{:S(2)}, u32[]{:S(2)}) async-start(bf16[128,2,512]{2,1,0:T(2,128)(2,1)} %reshape.47), calls=%async_computation.1 | async-start | bytes 524288 | tf_op jit(solution)/shard_map/all_to_all | solution.py:411
  48.2 3.3 %collective-permute-start.1 = (bf16[2,4,32,128]{3,2,1,0:T(8,128)(2,1)S(1)}, bf16[2,4,32,128]{3,2,1,0:T(8,128)(2,1)S(1)}, u32[]{:S(2)}, u32[]{:S(2)}) collective-permute-start(bf16[2,4,32,128]{3,2,1,0:T(8,128)(2,1)S(1)} %pad_maximum_fusion.1), channel_id=1, source_target_pairs={{0,2},{2,0},{4,6},{6,4},{8,10},{10,8},{12,14},{14,12},{1,3},{3,1},... | collective-permute-start | bytes 196616 | tf_op jit(solution)/shard_map/ppermute | solution.py:357
  51.5 4.0 %collective-permute-start.2 = (bf16[2,4,32,128]{3,2,1,0:T(8,128)(2,1)S(1)}, bf16[2,4,32,128]{3,2,1,0:T(8,128)(2,1)S(1)}, u32[]{:S(2)}, u32[]{:S(2)}) collective-permute-start(bf16[2,4,32,128]{3,2,1,0:T(8,128)(2,1)S(1)} %pad_maximum_fusion.1), channel_id=1, source_target_pairs={{0,4},{2,6},{4,0},{6,2},{8,12},{10,14},{12,8},{14,10},{1,5},{3,7},... | collective-permute-start | bytes 196616 | tf_op jit(solution)/shard_map/ppermute | solution.py:357
  55.5 2.0 %collective-permute-start.3 = (bf16[2,4,32,128]{3,2,1,0:T(8,128)(2,1)S(1)}, bf16[2,4,32,128]{3,2,1,0:T(8,128)(2,1)S(1)}, u32[]{:S(2)}, u32[]{:S(2)}) collective-permute-start(bf16[2,4,32,128]{3,2,1,0:T(8,128)(2,1)S(1)} %pad_maximum_fusion.1), channel_id=1, source_target_pairs={{0,6},{2,4},{4,2},{6,0},{8,14},{10,12},{12,10},{14,8},{1,7},{3,5},... | collective-permute-start | bytes 196616 | tf_op jit(solution)/shard_map/ppermute | solution.py:357
  57.6 0.5 collective-permute-done.2
  58.1 4.6 %collective-permute-done.3 = bf16[2,4,32,128]{3,2,1,0:T(8,128)(2,1)S(1)} collective-permute-done((bf16[2,4,32,128]{3,2,1,0:T(8,128)(2,1)S(1)}, bf16[2,4,32,128]{3,2,1,0:T(8,128)(2,1)S(1)}, u32[]{:S(2)}, u32[]{:S(2)}) %collective-permute-start.3) | collective-permute-done | bytes 65568 | tf_op jit(solution)/shard_map/ppermute | solution.py:357
  62.6 1.2 all-to-all-done.1
  63.8 0.1 broadcast_in_dim.10
  63.9 1.1 broadcast_in_dim.11
  65.0 3.5 %all-to-all-start.2 = ((bf16[4,256,512]{2,1,0:T(8,128)(2,1)}), bf16[4,256,512]{2,1,0:T(8,128)(2,1)S(1)}, u32[]{:S(2)}, u32[]{:S(2)}) async-start(bf16[4,256,512]{2,1,0:T(8,128)(2,1)} %broadcast_in_dim.11), calls=%async_computation.2 | async-start | bytes 2097152 | tf_op jit(solution)/shard_map/all_to_all | solution.py:361
  68.7 9.4 %prompt_attention.1 = bf16[1056,128]{1,0:T(8,128)(2,1)} custom-call(bf16[8,2,16,128]{3,2,1,0:T(8,128)(2,1)} %bitcast.48, bf16[8,2,16,128]{3,2,1,0:T(8,128)(2,1)} %bitcast.55, bf16[8,2,16,128]{3,2,1,0:T(8,128)(2,1)} %bitcast.56, bf16[8,2,16,128]{3,2,1,0:T(8,128)(2,1)} %bitcast.57, bf16[16,2,2,256,128]{4,3,2,1,0:T(8,128)(2,1)} %bitcast.52), custom_call_target="tpu_custom_call" | custom-call | flops 3221225472 | bytes 4718592 | tf_op jit(solution)/shard_map/prompt_attention/pallas_call | solution.py:93
  78.1 4.9 %all-to-all-done.2.rows_ref = bf16[4,256,512]{2,1,0:T(8,128)(2,1)S(1)} async-done(((bf16[4,256,512]{2,1,0:T(8,128)(2,1)}), bf16[4,256,512]{2,1,0:T(8,128)(2,1)S(1)}, u32[]{:S(2)}, u32[]{:S(2)}) %all-to-all-start.2) | async-done | bytes 1048608 | tf_op jit(solution)/shard_map/all_to_all | solution.py:361
  83.1 0.8 expert_act.1
  83.9 8.7 %all_to_all.30.act_ref = bf16[4,384,128]{2,1,0:T(8,128)(2,1)S(1)} all-to-all(bf16[4,384,128]{2,1,0:T(8,128)(2,1)S(1)} %expert_act.1), channel_id=1, replica_groups=mesh['x'=4,'z'=8,'y'=8,'c'=2] {'x'}, dimensions={0} | all-to-all | bytes 786432 | tf_op jit(solution)/shard_map/all_to_all | solution.py:361
  92.6 0.7 expert_out.1
  93.3 0.1 reshape.52
  93.4 30.8 %all_to_all.31 = bf16[128,2,512]{2,1,0:T(2,128)(2,1)S(1)} all-to-all(bf16[128,2,512]{2,1,0:T(2,128)(2,1)S(1)} %reshape.52), channel_id=1, replica_groups=mesh['x'=4,'z'=8,'y'=8,'c'=2] {'z','y','c'}, dimensions={0} | all-to-all | bytes 524288 | tf_op jit(solution)/shard_map/all_to_all | solution.py:361
  124.3 0.1 reshape.53
  124.4 0.1 fusion.1
  124.5 0.6 reshape.54
  125.2 3.3 %all-to-all-start.5 = ((bf16[4,4,512]{2,1,0:T(4,128)(2,1)}), bf16[4,4,512]{2,1,0:T(4,128)(2,1)S(1)}, u32[]{:S(2)}, u32[]{:S(2)}) async-start(bf16[4,4,512]{2,1,0:T(4,128)(2,1)} %reshape.54), calls=%async_computation.5 | async-start | bytes 32768 | tf_op jit(solution)/shard_map/all_to_all | solution.py:361
  128.5 2.8 %merge_partials.1 = bf16[128,128]{1,0:T(8,128)(2,1)} custom-call(s32[1]{0:T(128)} %bitcast.21.place_ref, bf16[8,1056,128]{2,1,0:T(8,128)(2,1)} %bitcast.46, f32[128,128]{1,0:T(8,128)} %get-tuple-element.40.suffix_ref, f32[1,128]{1,0:T(1,128)} %get-tuple-element.41.suffix_log_ref), custom_call_target="tpu_custom_call" | custom-call | flops 983040 | bytes 491520 | tf_op jit(solution)/shard_map/merge_partials/pallas_call | solution.py:154
  131.3 1.3 all-to-all-done.5
  132.6 0.6 maximum_bitcast_fusion
  (32 shorter events, 0.3 us)
Async XLA Ops:
  7.2 8.8 %copy-start.3 = (bf16[1,4,32,128]{3,2,1,0:T(8,128)(2,1)S(1)}, bf16[1,4,32,128]{3,2,1,0:T(8,128)(2,1)}, u32[]{:S(2)}) copy-start(bf16[1,4,32,128]{3,2,1,0:T(8,128)(2,1)} %param.12) | copy-start | bytes 98308
  7.2 18.2 %copy-start.4 = (bf16[1,4,32,128]{3,2,1,0:T(8,128)(2,1)S(1)}, bf16[1,4,32,128]{3,2,1,0:T(8,128)(2,1)}, u32[]{:S(2)}) copy-start(bf16[1,4,32,128]{3,2,1,0:T(8,128)(2,1)} %param.12) | copy-start | bytes 98308
  7.2 61.4 %all-gather.5.cloned.1.call-start = ((), (), s32[]{:S(2)}) async-start(), calls=%async_computation.6 | async-start | bytes 4456448 | tf_op jit(solution)/shard_map/all_gather | solution.py:388
  11.1 14.3 %all-to-all-start = ((bf16[4,200,512]{2,1,0:T(8,128)(2,1)}), bf16[4,200,512]{2,1,0:T(8,128)(2,1)S(1)}, u32[]{:S(2)}, u32[]{:S(2)}) async-start(bf16[4,200,512]{2,1,0:T(8,128)(2,1)} %columns_first.1), calls=%async_computation | async-start | bytes 1638400 | tf_op jit(solution)/shard_map/all_to_all | solution.py:361
  15.9 9.4 %collective-permute-start = (bf16[1,4,32,128]{3,2,1,0:T(8,128)(2,1)S(1)}, bf16[1,4,32,128]{3,2,1,0:T(8,128)(2,1)S(1)}, u32[]{:S(2)}, u32[]{:S(2)}) collective-permute-start(bf16[1,4,32,128]{3,2,1,0:T(8,128)(2,1)S(1)} %copy-done.3), channel_id=1, source_target_pairs={{0,8},{2,10},{4,12},{6,14},{8,0},{10,2},{12,4},{14,6},{1,9},{3,11}... | collective-permute-start | bytes 98312 | tf_op jit(solution)/shard_map/ppermute | solution.py:357
  25.4 43.2 %copy-start.2 = (bf16[2,4,32,128]{3,2,1,0:T(8,128)(2,1)}, bf16[2,4,32,128]{3,2,1,0:T(8,128)(2,1)S(1)}, u32[]{:S(2)}) copy-start(bf16[2,4,32,128]{3,2,1,0:T(8,128)(2,1)S(1)} %pad_maximum_fusion.1) | copy-start | bytes 196612
  27.2 36.6 %all-to-all-start.1 = ((bf16[128,2,512]{2,1,0:T(2,128)(2,1)}), bf16[128,2,512]{2,1,0:T(2,128)(2,1)S(1)}, u32[]{:S(2)}, u32[]{:S(2)}) async-start(bf16[128,2,512]{2,1,0:T(2,128)(2,1)} %reshape.47), calls=%async_computation.1 | async-start | bytes 524288 | tf_op jit(solution)/shard_map/all_to_all | solution.py:411
  48.2 9.3 %collective-permute-start.1 = (bf16[2,4,32,128]{3,2,1,0:T(8,128)(2,1)S(1)}, bf16[2,4,32,128]{3,2,1,0:T(8,128)(2,1)S(1)}, u32[]{:S(2)}, u32[]{:S(2)}) collective-permute-start(bf16[2,4,32,128]{3,2,1,0:T(8,128)(2,1)S(1)} %pad_maximum_fusion.1), channel_id=1, source_target_pairs={{0,2},{2,0},{4,6},{6,4},{8,10},{10,8},{12,14},{14,12},{1,3},{3,1},... | collective-permute-start | bytes 196616 | tf_op jit(solution)/shard_map/ppermute | solution.py:357
  51.5 6.5 %collective-permute-start.2 = (bf16[2,4,32,128]{3,2,1,0:T(8,128)(2,1)S(1)}, bf16[2,4,32,128]{3,2,1,0:T(8,128)(2,1)S(1)}, u32[]{:S(2)}, u32[]{:S(2)}) collective-permute-start(bf16[2,4,32,128]{3,2,1,0:T(8,128)(2,1)S(1)} %pad_maximum_fusion.1), channel_id=1, source_target_pairs={{0,4},{2,6},{4,0},{6,2},{8,12},{10,14},{12,8},{14,10},{1,5},{3,7},... | collective-permute-start | bytes 196616 | tf_op jit(solution)/shard_map/ppermute | solution.py:357
  55.5 7.1 %collective-permute-start.3 = (bf16[2,4,32,128]{3,2,1,0:T(8,128)(2,1)S(1)}, bf16[2,4,32,128]{3,2,1,0:T(8,128)(2,1)S(1)}, u32[]{:S(2)}, u32[]{:S(2)}) collective-permute-start(bf16[2,4,32,128]{3,2,1,0:T(8,128)(2,1)S(1)} %pad_maximum_fusion.1), channel_id=1, source_target_pairs={{0,6},{2,4},{4,2},{6,0},{8,14},{10,12},{12,10},{14,8},{1,7},{3,5},... | collective-permute-start | bytes 196616 | tf_op jit(solution)/shard_map/ppermute | solution.py:357
  57.5 11.1 %copy-start.6 = (bf16[2,4,32,128]{3,2,1,0:T(8,128)(2,1)}, bf16[2,4,32,128]{3,2,1,0:T(8,128)(2,1)S(1)}, u32[]{:S(2)}) copy-start(bf16[2,4,32,128]{3,2,1,0:T(8,128)(2,1)S(1)} %collective-permute-done.1) | copy-start | bytes 196612
  58.1 10.5 %copy-start.7 = (bf16[2,4,32,128]{3,2,1,0:T(8,128)(2,1)}, bf16[2,4,32,128]{3,2,1,0:T(8,128)(2,1)S(1)}, u32[]{:S(2)}) copy-start(bf16[2,4,32,128]{3,2,1,0:T(8,128)(2,1)S(1)} %collective-permute-done.2) | copy-start | bytes 196612
  62.6 6.0 %copy-start.8 = (bf16[2,4,32,128]{3,2,1,0:T(8,128)(2,1)}, bf16[2,4,32,128]{3,2,1,0:T(8,128)(2,1)S(1)}, u32[]{:S(2)}) copy-start(bf16[2,4,32,128]{3,2,1,0:T(8,128)(2,1)S(1)} %collective-permute-done.3) | copy-start | bytes 196612
  65.0 18.0 %all-to-all-start.2 = ((bf16[4,256,512]{2,1,0:T(8,128)(2,1)}), bf16[4,256,512]{2,1,0:T(8,128)(2,1)S(1)}, u32[]{:S(2)}, u32[]{:S(2)}) async-start(bf16[4,256,512]{2,1,0:T(8,128)(2,1)} %broadcast_in_dim.11), calls=%async_computation.2 | async-start | bytes 2097152 | tf_op jit(solution)/shard_map/all_to_all | solution.py:361
  68.5 59.9 %all-gather.7.cloned.1.call-start = ((), (), s32[]{:S(2)}) async-start(), calls=%async_computation.7 | async-start | bytes 2433024 | tf_op jit(solution)/shard_map/all_gather | solution.py:418
  68.6 14.4 %copy-start = (bf16[1,192,2048]{2,1,0:T(8,128)(2,1)S(1)}, bf16[1,192,2048]{2,1,0:T(8,128)(2,1)}, u32[]{:S(2)}) copy-start(bf16[1,192,2048]{2,1,0:T(8,128)(2,1)} %param.21) | copy-start | bytes 2359300
  68.6 14.4 %copy-start.1 = (bf16[1,192,2048]{2,1,0:T(8,128)(2,1)S(1)}, bf16[1,192,2048]{2,1,0:T(8,128)(2,1)}, u32[]{:S(2)}) copy-start(bf16[1,192,2048]{2,1,0:T(8,128)(2,1)} %param.22) | copy-start | bytes 2359300
  78.1 46.3 %copy-start.5 = (bf16[32,256]{1,0:T(8,128)(2,1)S(1)}, bf16[32,256]{1,0:T(8,128)(2,1)}, u32[]{:S(2)}) copy-start(bf16[32,256]{1,0:T(8,128)(2,1)} %get-tuple-element.28) | copy-start | bytes 49156
  125.2 7.4 %all-to-all-start.5 = ((bf16[4,4,512]{2,1,0:T(4,128)(2,1)}), bf16[4,4,512]{2,1,0:T(4,128)(2,1)S(1)}, u32[]{:S(2)}, u32[]{:S(2)}) async-start(bf16[4,4,512]{2,1,0:T(4,128)(2,1)} %reshape.54), calls=%async_computation.5 | async-start | bytes 32768 | tf_op jit(solution)/shard_map/all_to_all | solution.py:361
Sparse Core Ops, SparseCore 0:
  10.1 55.8 all-gather.4
  83.2 41.9 all-gather.6
